TPU v7x, 32 devices: a whole 2x2x4 slice. The times are simulated.
32 devices in a mesh: dom: 8 (over z, y), sub: 4 (over x, core).
Axes of the slice: x: 2, y: 2, z: 4, core: 2. Of those that a mesh axis runs over, the one named last changes fastest.
Arguments:
- modal_state: float32 [56, 9, 4096], P(None, None, ('dom', 'sub')), may hold values from -6 to 6
- cluster_id: int32 [4096], P(('dom', 'sub')), may hold values 0 or 1
- jacobian_id: int32 [4096], P(('dom', 'sub')), may hold values from 0 to 63
- face_neighbour: int32 [4, 4096], P(None, ('dom', 'sub')), may hold values from 0 to 288, as said below
- flux_index: int32 [4, 4096], P(None, ('dom', 'sub')), may hold values from 0 to 11, as said below
- send_list: int32 [5120], P(('dom', 'sub')), may hold values from 0 to 511, as said below
- derivative: float32 [3, 56, 56], replicated, may hold values from -1.25 to 1.25
- stiffness: float32 [3, 56, 56], replicated, may hold values from -0.75 to 0.75
- restriction: float32 [4, 21, 56], replicated, may hold values from -0.75 to 0.75
- lifting: float32 [4, 56, 21], replicated, may hold values from -1.25 to 1.25
- orientation: float32 [3, 21, 21], replicated, may hold values from -1.25 to 1.25
- star_matrix: float32 [64, 3, 9, 9], replicated, may hold values from -2 to 2
- flux_minus: float32 [64, 4, 9, 9], replicated, may hold values from -2 to 2
- flux_plus: float32 [64, 4, 9, 9], replicated, may hold values from -2 to 2
Outputs:
- new_state: float32 [56, 9, 4096], P(None, None, ('dom', 'sub'))
Inputs may be any that keep to these rules, and one draw needn't show every extreme that they name: `face_neighbour`: each device's 4 * 128 faces are all distinct between interior pairs, live ghost slots and faces without neighbour. Along dom the devices at both ends have empty outer blocks; some device fills a dom block of 64 slots and every dom group has two sub-blocks sharing 8 faces. For a face whose neighbour is in a ghost slot, flux_index // 3 equals the face number listed in the sender's send_list slot divided by 128. `send_list`: the first 160 faces of a permutation of each device's 4 * 128 faces; slots past a link's count list faces without a neighbour.
All inputs are finite; a program needn't handle non-finite values. No bound on the sum of `cluster_id` on one device may be relied on, other than what follows from the above.
Results may differ from a plain program's by a relative error of at most 0.0003.
Values sent between devices are 32-bit elements; how exact they have to be, the bound alone decides.
No kernel may reach another device: no remote copies, remote signals or barrier semaphores. Data moves between devices by JAX's collectives and lax.ppermute only.
A program may use at most 64 MiB of HBM per device.

v0:
```python
import collections
import functools

import jax
import jax.numpy as jnp
from jax import lax
from jax.experimental import pallas as pl
from jax.experimental.pallas import tpu as pltpu
from jax.sharding import PartitionSpec as P

ORDER = 6
CAP_DOM = 64
HALF = 0.5
PAD = 24
SEC = 64
OSEC = 32
GROUP = 3

F32 = jnp.float32
BF16 = jnp.bfloat16
I32 = jnp.int32

Sizes = collections.namedtuple(
    "Sizes", ["variables", "basis", "sub_count", "cap_sub", "rows", "half_rows"]
)


def split(x):
    high = x.astype(BF16)
    low = (x - high.astype(F32)).astype(BF16)
    return high, low


def dot(a, b):
    return lax.dot_general(a, b, (((1,), (0,)), ((), ())), preferred_element_type=F32)


def dot_nt(a, b):
    return lax.dot_general(a, b, (((1,), (1,)), ((), ())), preferred_element_type=F32)


def pad_to(x, rows, lanes):
    m, k = x.shape
    if lanes > k:
        x = jnp.concatenate([x, jnp.zeros((m, lanes - k), x.dtype)], axis=1)
    if rows > m:
        x = jnp.concatenate([x, jnp.zeros((rows - m, lanes), x.dtype)], axis=0)
    return x


def stack_left(matrix):
    m = -(-matrix.shape[0] // 16) * 16
    wide = pad_to(matrix, m, 128)
    high = wide.astype(BF16).astype(F32)
    low = wide - high
    both = high + pltpu.roll(high, SEC, 1)
    return jnp.concatenate([both.astype(BF16), low.astype(BF16)], axis=1)[:, : 3 * SEC]


def stack_right(blocks):
    out = []
    for x in blocks:
        high, low = split(pad_to(x, SEC, x.shape[1]))
        out.append(jnp.concatenate([high, low, high], axis=0))
    return jnp.concatenate(out, axis=1) if len(out) > 1 else out[0]


def mix_group(moved_ref, star_ref, sizes, g):
    basis, variables = sizes.basis, sizes.variables
    acc = [None] * GROUP
    for q in range(variables):
        for d in range(3):
            block = moved_ref[d * basis : (d + 1) * basis, q * 128 : (q + 1) * 128]
            for i in range(GROUP):
                row = (q * variables + g * GROUP + i) * 4 + d
                term = block * star_ref[row : row + 1, :]
                acc[i] = term if acc[i] is None else acc[i] + term
    return acc


def lookup(table_ref, stage_ref, class_row, out_ref):
    nq, np_, parts, classes = table_ref.shape
    for q in range(nq):
        for p in range(np_):
            row = (q * np_ + p) * 4
            stage_ref[row : row + parts, :classes] = table_ref[q, p]
    rows = stage_ref.shape[0]
    high, low = split(stage_ref[:, :classes])
    onehot = (lax.broadcasted_iota(I32, (classes, 128), 0) == class_row).astype(F32).astype(BF16)
    out_ref[0:rows, :] = dot(high, onehot) + dot(low, onehot)


def groups(sizes):
    return range(sizes.variables // GROUP)


def group_lanes(g):
    return slice(g * GROUP * 128, (g + 1) * GROUP * 128)


def advance(src_ref, dst_ref, star_ref, left, sizes, emit):
    for g in groups(sizes):
        acc = mix_group(src_ref, star_ref, sizes, g)
        for i in range(GROUP):
            emit(g * GROUP + i, acc[i])
        dst_ref[:, group_lanes(g)] = dot(left, stack_right(acc))[: dst_ref.shape[0]]


def predictor(moved_ref, other_ref, star_ref, left, first_ref, late_ref, sizes, finish):
    def weigh(weights, degree):
        w_half, w_full = weights
        scale = -1.0 / (degree + 1).astype(F32)
        return w_half * (scale * HALF), w_full * scale

    def emitter(weights):
        w_half, w_full = weights

        def emit(p, value):
            first_ref[p] += w_half * value
            if late_ref is not None:
                late_ref[p] += (w_full - w_half) * value

        return emit

    def two(i, weights):
        weights = weigh(weights, 2 * i + 1)
        advance(moved_ref, other_ref, star_ref, left, sizes, emitter(weights))
        weights = weigh(weights, 2 * i + 2)
        advance(other_ref, moved_ref, star_ref, left, sizes, emitter(weights))
        return weights

    steps = ORDER - 1
    weights = lax.fori_loop(0, steps // 2, two, (jnp.float32(HALF), jnp.float32(1.0)))
    w_half, w_full = weigh(weights, jnp.int32(steps))
    for g in groups(sizes):
        acc = mix_group(moved_ref, star_ref, sizes, g)
        values = []
        for i in range(GROUP):
            p = g * GROUP + i
            first = first_ref[p] + w_half * acc[i]
            if late_ref is not None:
                late_ref[p] += (w_full - w_half) * acc[i]
            values.append(finish(p, first))
        yield g, values


def project(g, values, left, proj_ref):
    proj_ref[:, group_lanes(g)] = dot(left, stack_right(values))


def by_face(proj_ref, faces_ref, sizes):
    rows = sizes.rows
    for f in range(4):
        pieces = [
            proj_ref[f * PAD : (f + 1) * PAD, q * 128 : (q + 1) * 128] for q in range(sizes.variables)
        ]
        high, low = split(pad_to(jnp.concatenate(pieces, axis=0), rows, 128))
        faces_ref[0:rows, f * 128 : (f + 1) * 128] = high
        faces_ref[rows : 2 * rows, f * 128 : (f + 1) * 128] = low


def is_even():
    return lax.rem(lax.axis_index("dom"), 2) == 0


def low_lanes(shape):
    return lax.broadcasted_iota(I32, shape, 1) < CAP_DOM


def picks_of_sends(send_ref, pick_ref, pick_sub_ref):
    ghosts = send_ref.shape[1]
    row = send_ref[...].astype(F32)
    dom_row = row[:, 0:128]
    dom_row = jnp.where(is_even(), pltpu.roll(dom_row, CAP_DOM, 1), dom_row)
    place = lax.broadcasted_iota(I32, (128, 128), 0).astype(F32)
    for f in range(4):
        pick_ref[f * 128 : (f + 1) * 128, :] = (place + f * 128 == dom_row).astype(F32).astype(BF16)
    subs = ghosts - 128
    sub_row = pad_to(row[:, 128:], 1, 128)
    column = jnp.transpose(jnp.broadcast_to(sub_row, (128, 128)), (1, 0))[:subs]
    lane = lax.broadcasted_iota(I32, (subs, 128), 1).astype(F32)
    for f in range(4):
        pick_sub_ref[:, f * 128 : (f + 1) * 128] = (column == lane + f * 128).astype(F32).astype(BF16)


def payloads(faces_ref, pick_ref, pick_sub_ref, slot_ref, outs, sizes):
    pa_ref, pb_ref, p1_ref, pk_refs = outs
    rows, half = sizes.rows, sizes.half_rows
    sub = dot_nt(pick_sub_ref[...], faces_ref[0:rows, :]) + dot_nt(pick_sub_ref[...], faces_ref[rows : 2 * rows, :])
    slot_ref[...] = pad_to(sub, sub.shape[0], slot_ref.shape[1])
    both = dot(faces_ref[...], pick_ref[...])
    both = both[0:rows] + both[rows : 2 * rows]
    top, bottom = both[0:half], both[half:]
    low = low_lanes((half, 128))
    pa_ref[...] = jnp.where(low, top, pltpu.roll(bottom, CAP_DOM, 1))
    pb_ref[...] = jnp.where(low, pltpu.roll(top, CAP_DOM, 1), bottom)
    me = lax.axis_index("sub")
    cap = sizes.cap_sub

    def block(k):
        return slot_ref[pl.ds(pl.multiple_of(jnp.bitwise_xor(me, k) * cap, 8), cap), :]

    p1_ref[0:cap, :] = block(1)
    for i, k in enumerate(range(2, sizes.sub_count, 2)):
        p1_ref[(i + 1) * cap : (i + 2) * cap, :] = block(k + 1)
        pk_refs[i][...] = block(k)


def unpack(ins, slot_ref, sizes):
    ra_ref, rb_ref, r1_ref, rk_refs = ins
    ra, rb = ra_ref[...], rb_ref[...]
    low = low_lanes(ra.shape)
    top = jnp.where(low, ra, pltpu.roll(rb, CAP_DOM, 1))
    bottom = jnp.where(low, pltpu.roll(ra, CAP_DOM, 1), rb)
    dom = jnp.concatenate([top, bottom], axis=0)
    me = lax.axis_index("sub")
    cap = sizes.cap_sub
    slot_ref[...] = jnp.zeros_like(slot_ref)

    def put(k, value):
        slot_ref[pl.ds(pl.multiple_of(jnp.bitwise_xor(me, k) * cap, 8), cap), :] = value

    put(1, r1_ref[0:cap, :])
    for i, k in enumerate(range(2, sizes.sub_count, 2)):
        put(k, rk_refs[i][0:cap, :])
        put(k + 1, rk_refs[i][cap : 2 * cap, :])
    sub = jnp.transpose(slot_ref[...], (1, 0))[: dom.shape[0]]
    return jnp.concatenate([dom, sub], axis=1)


def turn_blocks(values, left, turns):
    out = []
    for value in values:
        high, low = split(pad_to(value, OSEC, value.shape[1]))
        turned = dot(left, jnp.concatenate([high, low, high], axis=0))
        out.append(
            jnp.where(
                turns == 0,
                turned[0:PAD],
                jnp.where(turns == 1, turned[PAD : 2 * PAD], turned[2 * PAD : 3 * PAD]),
            )
        )
    return out


def orient_left(orient_ref):
    blocks = [pad_to(orient_ref[h], PAD, 128) for h in range(3)]
    wide = pad_to(jnp.concatenate(blocks, axis=0), 80, 128)
    high = wide.astype(BF16).astype(F32)
    low = wide - high
    stacked = high + pltpu.roll(high, OSEC, 1) + pltpu.roll(low, 2 * OSEC, 1)
    return stacked.astype(BF16)[:, : 3 * OSEC]


def face_of(flux):
    return (flux >= 3).astype(I32) + (flux >= 6).astype(I32) + (flux >= 9).astype(I32)


def kernel_predict(sizes, *refs):
    xs = sizes.sub_count // 2 - 1
    (state_hbm, class_hbm, table_hbm, deriv_hbm, restrict_hbm, send_hbm, *later_hbm) = refs[:14]
    refs = refs[14:]
    class_ref, refs = refs[0], refs[1:]
    later_refs, refs = refs[:8], refs[8:]
    (state_ref, first_ref, late_ref, proj_ref, faces_ref, star_ref, dleft_ref, rleft_ref, pick_ref, pick_sub_ref,
     pa_ref, pb_ref, p1_ref, *rest) = refs
    pk_refs, rest = rest[:xs], rest[xs:]
    (table_ref, deriv_ref, restrict_ref, send_ref, moved_ref, other_ref, stage_ref, rstage_ref, slot_ref,
     sems) = rest
    sources = [class_hbm, table_hbm, deriv_hbm, state_hbm, send_hbm, restrict_hbm, *later_hbm]
    targets = [class_ref, table_ref, deriv_ref, state_ref, send_ref, restrict_ref, *later_refs]
    copies = [pltpu.make_async_copy(s, t, sems.at[i]) for i, (s, t) in enumerate(zip(sources, targets))]
    for copy in copies:
        copy.start()
    variables, basis = sizes.variables, sizes.basis
    copies[0].wait()
    copies[1].wait()
    lookup(table_ref, stage_ref, class_ref[...], star_ref)
    copies[2].wait()
    dleft_ref[...] = stack_left(jnp.reshape(deriv_ref[...], (3 * basis, basis)))
    left = dleft_ref[...]
    copies[3].wait()
    for g in groups(sizes):
        values = [state_ref[g * GROUP + i] for i in range(GROUP)]
        moved_ref[:, group_lanes(g)] = dot(left, stack_right(values))[: moved_ref.shape[0]]
        for i in range(GROUP):
            first_ref[g * GROUP + i] = values[i] * HALF
            late_ref[g * GROUP + i] = values[i] * (1.0 - HALF)
    copies[4].wait()
    picks_of_sends(send_ref, pick_ref, pick_sub_ref)
    copies[5].wait()
    faces, face_basis = 4, restrict_ref.shape[0]
    rstage_ref[...] = jnp.zeros_like(rstage_ref)
    for f in range(faces):
        rstage_ref[f * PAD : f * PAD + face_basis, :basis] = restrict_ref[:, f, :]
    rleft_ref[...] = stack_left(rstage_ref[:, :basis])

    def finish(p, first):
        first_ref[p] = first
        return first

    for g, values in predictor(moved_ref, other_ref, star_ref, left, first_ref, late_ref, sizes, finish):
        project(g, values, rleft_ref[...], proj_ref)
    by_face(proj_ref, faces_ref, sizes)
    payloads(faces_ref, pick_ref, pick_sub_ref, slot_ref, (pa_ref, pb_ref, p1_ref, pk_refs), sizes)
    for copy in copies[6:]:
        copy.wait()


def volume_part(values_ref, base_ref, star_ref, kleft, moved_ref, partial_ref, sizes):
    for g in groups(sizes):
        values = [values_ref[g * GROUP + i] for i in range(GROUP)]
        moved_ref[:, group_lanes(g)] = dot(kleft, stack_right(values))[: moved_ref.shape[0]]
    for g in groups(sizes):
        acc = mix_group(moved_ref, star_ref, sizes, g)
        for i in range(GROUP):
            partial_ref[g * GROUP + i] = base_ref[g * GROUP + i] + acc[i]


def interior_part(faces_ref, pick_ref, oleft, turn, gath_ref, sizes):
    rows = sizes.rows
    both = dot(faces_ref[...], pick_ref[...])
    both = both[0:rows] + both[rows : 2 * rows]
    blocks = [both[q * PAD : (q + 1) * PAD] for q in range(sizes.variables)]
    for q, block in enumerate(turn_blocks(blocks, oleft, turn)):
        gath_ref[q * PAD : (q + 1) * PAD, :] = block


def own_part(proj_ref, minus_ref, comb_ref, sizes):
    variables = sizes.variables
    for f in range(4):
        rows = slice(f * PAD, (f + 1) * PAD)
        acc = [None] * variables
        for q in range(variables):
            block = proj_ref[rows, q * 128 : (q + 1) * 128]
            for p in range(variables):
                row = (q * variables + p) * 4 + f
                term = block * minus_ref[row : row + 1, :]
                acc[p] = term if acc[p] is None else acc[p] + term
        for p in range(variables):
            comb_ref[rows, p * 128 : (p + 1) * 128] = acc[p]


def kernel_local_first(sizes, *refs):
    (class_ref, minus_table, plus_table, code_ref, flux_ref, stiff_ref, lift_ref, orient_ref,
     first_ref, state_ref, star_ref, proj_ref, faces_ref,
     partial_ref, gath_ref, comb_ref, minus_ref, plus_ref, kleft_ref, oleft_ref, lleft_ref, llow_ref,
     pick_ref, ghost_pick_ref, turn_ref, ghost_turn_ref, moved_ref, stage_ref, lstage_ref) = refs
    basis = sizes.basis
    kleft_ref[...] = stack_left(jnp.reshape(stiff_ref[...], (3 * basis, basis)))
    volume_part(first_ref, state_ref, star_ref, kleft_ref[...], moved_ref, partial_ref, sizes)
    lookup(minus_table, stage_ref, class_ref[...], minus_ref)
    oleft_ref[...] = orient_left(orient_ref)
    code = code_ref[...]
    flux = flux_ref[...]
    face = face_of(flux)
    turn = flux - 3 * face
    turn_row = jnp.concatenate([turn[f : f + 1, :] for f in range(4)], axis=1)
    turn_ref[...] = turn_row
    place = lax.broadcasted_iota(I32, (128, 128), 0)
    target = jnp.where(code < 128, face * 128 + code, -1)
    for f in range(4):
        for j in range(4):
            pick_ref[j * 128 : (j + 1) * 128, f * 128 : (f + 1) * 128] = (
                (place + j * 128 == target[f : f + 1, :]).astype(F32).astype(BF16)
            )
    slot = code - 128
    swapped = jnp.where(slot < CAP_DOM, slot + CAP_DOM, jnp.where(slot < 2 * CAP_DOM, slot - CAP_DOM, slot))
    slot = jnp.where(is_even(), swapped, slot)
    slot = jnp.where(code < 128, -1, slot)
    for f in range(4):
        for j in range(2):
            ghost_pick_ref[j * 128 : (j + 1) * 128, f * 128 : (f + 1) * 128] = (
                (place + j * 128 == slot[f : f + 1, :]).astype(F32).astype(BF16)
            )
    rows = jnp.broadcast_to(turn_row.astype(F32), (16, 512)).astype(BF16)
    ghost_turn_ref[...] = dot_nt(rows, ghost_pick_ref[...])[0:1].astype(I32)
    interior_part(faces_ref, pick_ref, oleft_ref[...], turn_row, gath_ref, sizes)
    own_part(proj_ref, minus_ref, comb_ref, sizes)
    lookup(plus_table, stage_ref, class_ref[...], plus_ref)
    lstage_ref[...] = jnp.zeros_like(lstage_ref)
    for f in range(4):
        lstage_ref[f * PAD : f * PAD + lift_ref.shape[0], :basis] = lift_ref[:, f, :]
    wide = jnp.transpose(lstage_ref[...], (1, 0))[:64]
    high = wide.astype(BF16).astype(F32)
    low = wide - high
    rolled = pltpu.roll(high, 4 * PAD, 1)
    lane = lax.broadcasted_iota(I32, (64, 128), 1)
    lleft_ref[:, 0:128] = jnp.where(lane < 4 * PAD, high, rolled).astype(BF16)
    lleft_ref[:, 128:256] = jnp.where(lane < 8 * PAD - 128, rolled, 0.0).astype(BF16)
    llow_ref[...] = low.astype(BF16)


def kernel_local_second(sizes, *refs):
    (second_ref, middle_ref, star_ref, kleft_ref, proj_ref, faces_ref, minus_ref, oleft_ref, pick_ref, turn_ref,
     partial_ref, gath_ref, comb_ref, moved_ref) = refs
    volume_part(second_ref, middle_ref, star_ref, kleft_ref[...], moved_ref, partial_ref, sizes)
    interior_part(faces_ref, pick_ref, oleft_ref[...], turn_ref[...], gath_ref, sizes)
    own_part(proj_ref, minus_ref, comb_ref, sizes)


def neighbour_part(ins, oleft_ref, ghost_turn_ref, ghost_pick_ref, gath_ref, comb_ref, plus_ref, lleft_ref, llow_ref,
                   partial_ref, slot_ref, ghost_ref, gsum_ref, sizes):
    variables, basis, rows = sizes.variables, sizes.basis, sizes.rows
    received = unpack(ins, slot_ref, sizes)
    blocks = [received[q * PAD : (q + 1) * PAD] for q in range(variables)]
    turned = turn_blocks(blocks, oleft_ref[...], ghost_turn_ref[...])
    high, low = split(pad_to(jnp.concatenate(turned, axis=0), rows, turned[0].shape[1]))
    ghost_ref[0:rows, :] = high
    ghost_ref[rows : 2 * rows, :] = low
    both = dot(ghost_ref[...], ghost_pick_ref[...])
    used = variables * PAD
    gsum_ref[...] = gath_ref[...] + (both[0:used] + both[rows : rows + used])
    for g in groups(sizes):
        highs, stacks = [], []
        faces = [[], [], []]
        for f in range(4):
            frows = slice(f * PAD, (f + 1) * PAD)
            acc = []
            for i in range(GROUP):
                p = g * GROUP + i
                acc.append(comb_ref[frows, p * 128 : (p + 1) * 128])
            for q in range(variables):
                block = gsum_ref[q * PAD : (q + 1) * PAD, f * 128 : (f + 1) * 128]
                for i in range(GROUP):
                    row = (q * variables + g * GROUP + i) * 4 + f
                    acc[i] = acc[i] + block * plus_ref[row : row + 1, :]
            for i in range(GROUP):
                faces[i].append(acc[i])
        for i in range(GROUP):
            high, low = split(jnp.concatenate(faces[i], axis=0))
            highs.append(high)
            stacks.append(jnp.concatenate([high, low], axis=0))
        lifted = dot(lleft_ref[:, : 8 * PAD], jnp.concatenate(stacks, axis=1)) + dot(
            llow_ref[:, : 4 * PAD], jnp.concatenate(highs, axis=1)
        )
        yield g, [
            partial_ref[g * GROUP + i] + lifted[:basis, i * 128 : (i + 1) * 128] for i in range(GROUP)
        ]


def kernel_second(sizes, *refs):
    xs = sizes.sub_count // 2 - 1
    ra_ref, rb_ref, r1_ref, *refs = refs
    rk_refs, refs = refs[:xs], refs[xs:]
    (oleft_ref, ghost_turn_ref, ghost_pick_ref, gath_ref, comb_ref, plus_ref, lleft_ref, llow_ref, partial_ref,
     star_ref, late_ref, cluster_ref, dleft_ref, rleft_ref, pick_ref, pick_sub_ref,
     middle_ref, second_ref, proj_ref, faces_ref, pa_ref, pb_ref, p1_ref, *rest) = refs
    pk_refs, rest = rest[:xs], rest[xs:]
    moved_ref, other_ref, slot_ref, pslot_ref, ghost_ref, gsum_ref = rest
    left = dleft_ref[...]
    for g, values in neighbour_part((ra_ref, rb_ref, r1_ref, rk_refs), oleft_ref, ghost_turn_ref, ghost_pick_ref,
                                    gath_ref, comb_ref, plus_ref, lleft_ref, llow_ref, partial_ref, slot_ref,
                                    ghost_ref, gsum_ref, sizes):
        moved_ref[:, group_lanes(g)] = dot(left, stack_right(values))[: moved_ref.shape[0]]
        for i in range(GROUP):
            middle_ref[g * GROUP + i] = values[i]
            second_ref[g * GROUP + i] = values[i] * HALF
    fine = cluster_ref[...] == 1

    def finish(p, first):
        value = jnp.where(fine, first, late_ref[p])
        second_ref[p] = value
        return value

    for g, values in predictor(moved_ref, other_ref, star_ref, left, second_ref, None, sizes, finish):
        project(g, values, rleft_ref[...], proj_ref)
    by_face(proj_ref, faces_ref, sizes)
    payloads(faces_ref, pick_ref, pick_sub_ref, pslot_ref, (pa_ref, pb_ref, p1_ref, pk_refs), sizes)


def kernel_last(sizes, *refs):
    xs = sizes.sub_count // 2 - 1
    ra_ref, rb_ref, r1_ref, *refs = refs
    rk_refs, refs = refs[:xs], refs[xs:]
    (oleft_ref, ghost_turn_ref, ghost_pick_ref, gath_ref, comb_ref, plus_ref, lleft_ref, llow_ref, partial_ref,
     out_ref, slot_ref, ghost_ref, gsum_ref) = refs
    for g, values in neighbour_part((ra_ref, rb_ref, r1_ref, rk_refs), oleft_ref, ghost_turn_ref, ghost_pick_ref,
                                    gath_ref, comb_ref, plus_ref, lleft_ref, llow_ref, partial_ref, slot_ref,
                                    ghost_ref, gsum_ref, sizes):
        for i in range(GROUP):
            out_ref[g * GROUP + i] = values[i]


def body(
    dom_count,
    sub_count,
    modal_state,
    cluster_id,
    jacobian_id,
    face_neighbour,
    flux_index,
    send_list,
    derivative,
    stiffness,
    restriction,
    lifting,
    orientation,
    star_matrix,
    flux_minus,
    flux_plus,
):
    basis, variables, elements = modal_state.shape
    ghosts = send_list.shape[0]
    cap_sub = (ghosts - 2 * CAP_DOM) // sub_count
    lanes = variables * elements
    half_rows = -(-variables * PAD // 32) * 16
    rows = 2 * half_rows
    sizes = Sizes(variables, basis, sub_count, cap_sub, rows, half_rows)
    sub_lanes = -(-rows // 128) * 128
    mat_rows = variables * variables * 4 + 4
    xs = sub_count // 2 - 1

    state = jnp.transpose(modal_state, (1, 0, 2))
    star_table = jnp.transpose(star_matrix, (2, 3, 1, 0))
    minus_table = jnp.transpose(flux_minus, (2, 3, 1, 0))
    plus_table = jnp.transpose(flux_plus, (2, 3, 1, 0))
    restrict = jnp.transpose(restriction, (1, 0, 2))
    lift = jnp.transpose(lifting, (2, 0, 1))
    classes = jacobian_id.reshape(1, elements)
    clusters = cluster_id.reshape(1, elements)
    sends = send_list.reshape(1, ghosts)

    def sds(*shape, dtype=F32):
        return jax.ShapeDtypeStruct(shape, dtype)

    def like(x):
        return sds(*x.shape, dtype=x.dtype)

    whole = sds(variables, basis, elements)
    face_t = sds(4 * PAD, lanes)
    faces_t = sds(2 * rows, 4 * elements, dtype=BF16)
    mat_t = sds(mat_rows, 128)
    gath_t = sds(variables * PAD, 4 * elements)
    left_t = sds(-(-3 * basis // 16) * 16, 3 * SEC, dtype=BF16)
    pay_t = [sds(half_rows, 128)] * 2 + [sds(cap_sub * (xs + 1), sub_lanes)] + [sds(cap_sub, sub_lanes)] * xs

    def scratch(t):
        return pltpu.VMEM(t.shape, t.dtype)

    moved_s = pltpu.VMEM((3 * basis, lanes), F32)
    stage_s = pltpu.VMEM((mat_rows, 128), F32)
    slot_s = pltpu.VMEM((128, sub_lanes), F32)
    pslot_s = pltpu.VMEM((ghosts - 2 * CAP_DOM, sub_lanes), F32)
    ghost_s = pltpu.VMEM((2 * rows, 256), BF16)

    def call(fn, outs, scratches, operands, flops, space=pltpu.VMEM):
        vmem = pl.BlockSpec(memory_space=pltpu.VMEM)
        if space is pltpu.HBM:
            operands = [pltpu.with_memory_space_constraint(x, pltpu.HBM) for x in operands]
        return pl.pallas_call(
            functools.partial(fn, sizes),
            out_shape=outs,
            in_specs=[pl.BlockSpec(memory_space=space)] * len(operands),
            out_specs=jax.tree.map(lambda _: vmem, outs),
            scratch_shapes=scratches,
            cost_estimate=pl.CostEstimate(flops=flops, bytes_accessed=2_000_000, transcendentals=0),
            compiler_params=pltpu.CompilerParams(vmem_limit_bytes=24 * 1024 * 1024),
        )(*operands)

    combined = ("dom", "sub")

    def device(d, s):
        return d * sub_count + s

    def pairs(target):
        return [(device(d, s), device(*target(d, s))) for d in range(dom_count) for s in range(sub_count)]

    even_pairs = pairs(lambda d, s: (d ^ 1, s))
    odd_pairs = pairs(lambda d, s: (((d + 1) ^ 1) - 1, s) if 0 < d < dom_count - 1 else (d, s ^ 1))

    def sub_pairs(k):
        return pairs(lambda d, s: (d, s ^ k))

    def trade(payload):
        pa, pb, p1, *pk = payload
        r1 = lax.ppermute(p1, combined, sub_pairs(1))
        rb = lax.ppermute(pb, combined, odd_pairs)
        ra = lax.ppermute(pa, combined, even_pairs)
        rk = []
        for i, part in enumerate(pk):
            passed = r1[(i + 1) * cap_sub : (i + 2) * cap_sub]
            rk.append(lax.ppermute(jnp.concatenate([part, passed], axis=0), combined, sub_pairs(2 * i + 2)))
        return [ra, rb, r1, *rk]

    later = [clusters, minus_table, plus_table, face_neighbour, flux_index, stiffness, lift, orientation]
    outs = call(
        kernel_predict,
        [like(x) for x in [classes, *later]]
        + [whole, whole, whole, face_t, faces_t, mat_t, left_t, sds(4 * PAD, 3 * SEC, dtype=BF16)]
        + [sds(4 * elements, 128, dtype=BF16), sds(ghosts - 2 * CAP_DOM, 4 * elements, dtype=BF16)]
        + pay_t,
        [
            scratch(star_table), scratch(derivative), scratch(restrict), scratch(sends),
            moved_s, moved_s, stage_s, pltpu.VMEM((4 * PAD, 128), F32), pslot_s, pltpu.SemaphoreType.DMA((14,)),
        ],
        [state, classes, star_table, derivative, restrict, sends, *later],
        60_000_000,
        pltpu.HBM,
    )
    clusters, minus_table, plus_table, code, flux, stiff, lift, orient = outs[1:9]
    classes = outs[0]
    state, first, late, proj, faces, star, dleft, rleft, pick_send, pick_sub, *payload = outs[9:]
    received = trade(payload)
    (partial, gath, comb, minus, plus, kleft, oleft, lleft, llow, pick, ghost_pick, turn, ghost_turn) = call(
        kernel_local_first,
        [whole, gath_t, face_t, mat_t, mat_t, left_t, sds(80, 3 * OSEC, dtype=BF16)]
        + [sds(64, 256, dtype=BF16), sds(64, 128, dtype=BF16)]
        + [sds(4 * elements, 4 * elements, dtype=BF16), sds(256, 4 * elements, dtype=BF16)]
        + [sds(1, 4 * elements, dtype=I32), sds(1, 256, dtype=I32)],
        [moved_s, stage_s, pltpu.VMEM((128, 128), F32)],
        [classes, minus_table, plus_table, code, flux, stiff, lift, orient, first, state, star, proj, faces],
        30_000_000,
    )
    common = [oleft, ghost_turn, ghost_pick]
    middle, second, proj, faces, *payload = call(
        kernel_second,
        [whole, whole, face_t, faces_t] + pay_t,
        [moved_s, moved_s, slot_s, pslot_s, ghost_s, scratch(gath_t)],
        received
        + common
        + [gath, comb, plus, lleft, llow, partial, star, late, clusters, dleft, rleft, pick_send, pick_sub],
        70_000_000,
    )
    received = trade(payload)
    partial, gath, comb = call(
        kernel_local_second,
        [whole, gath_t, face_t],
        [moved_s],
        [second, middle, star, kleft, proj, faces, minus, oleft, pick, turn],
        30_000_000,
    )
    result = call(
        kernel_last,
        whole,
        [slot_s, ghost_s, scratch(gath_t)],
        received + common + [gath, comb, plus, lleft, llow, partial],
        10_000_000,
    )
    return jnp.transpose(result, (1, 0, 2))


def solution(mesh):
    placed = (
        P(None, None, ("dom", "sub")),
        P(("dom", "sub")),
        P(("dom", "sub")),
        P(None, ("dom", "sub")),
        P(None, ("dom", "sub")),
        P(("dom", "sub")),
        P(),
        P(),
        P(),
        P(),
        P(),
        P(),
        P(),
        P(),
    )
    return jax.shard_map(
        functools.partial(body, mesh.shape["dom"], mesh.shape["sub"]),
        mesh=mesh,
        in_specs=placed,
        out_specs=P(None, None, ("dom", "sub")),
        check_vma=False,
    )
```

profile of v0, /device:TPU:0, one launch (start us, length us, event | category | flops | bytes accessed | tf_op | source)
XLA Modules:
  0.0 28.0 jit_solution(11623166371403987733)
XLA Ops:
  0.0 6.3 %shard_map.136 = (s32[1,128]{1,0:T(1,128)S(1)}, s32[1,128]{1,0:T(1,128)S(1)}, f32[9,9,4,64]{3,2,1,0:T(4,128)S(1)}, f32[9,9,4,64]{3,2,1,0:T(4,128)S(1)}, s32[4,12...) custom-call(f32[9,56,128]{2,1,0:T(8,128)} %bitcast.10, ...), custom_call_target="tpu_custom_call" | custom-call | flops 60000000 | bytes 2000000 | tf_op jit(solution)/shard_map/pallas_call | solution.py:551
  6.4 0.5 %collective-permute-start.2 = (f32[16,256]{1,0:T(8,128)S(1)}, f32[16,256]{1,0:T(8,128)S(1)}, u32[]{:S(2)}, u32[]{:S(2)}) collective-permute-start(f32[16,256]{1,0:T(8,128)S(1)} %get-tuple-element.54), channel_id=1, source_target_pairs={{0,1},{1,0},{2,3},{3,2},{4,5},{5,4},{6,7},{7,6},{8,9},{9,8},{10,11... | collective-permute-start | bytes 49160 | tf_op jit(solution)/shard_map/ppermute | solution.py:577
  6.9 2.6 %collective-permute-start = (f32[112,128]{1,0:T(8,128)S(1)}, f32[112,128]{1,0:T(8,128)S(1)}, u32[]{:S(2)}, u32[]{:S(2)}) collective-permute-start(f32[112,128]{1,0:T(8,128)S(1)} %get-tuple-element.52), channel_id=1, source_target_pairs={{0,4},{1,5},{2,6},{3,7},{4,0},{5,1},{6,2},{7,3},{8,12},{9,13},{10,... | collective-permute-start | bytes 172040 | tf_op jit(solution)/shard_map/ppermute | solution.py:579
  9.5 0.2 collective-permute-start.1
  9.6 0.0 collective-permute-done.2.refs_2_
  9.6 1.5 %collective-permute-start.3 = (f32[16,256]{1,0:T(8,128)S(1)}, f32[16,256]{1,0:T(8,128)S(1)}, u32[]{:S(2)}, u32[]{:S(2)}) collective-permute-start(f32[16,256]{1,0:T(8,128)S(1)} %pad_maximum_fusion), channel_id=1, source_target_pairs={{0,2},{1,3},{2,0},{3,1},{4,6},{5,7},{6,4},{7,5},{8,10},{9,11},{10,... | collective-permute-start | bytes 49160 | tf_op jit(solution)/shard_map/ppermute | solution.py:583
  11.2 2.3 %shard_map.137 = (f32[9,56,128]{2,1,0:T(8,128)S(1)}, f32[216,512]{1,0:T(8,128)S(1)}, f32[96,1152]{1,0:T(8,128)S(1)}, f32[328,128]{1,0:T(8,128)S(1)}, f32[328,128...) custom-call(s32[1,128]{1,0:T(1,128)S(1)} %get-tuple-element.56.refs_, ...), custom_call_target="tpu_custom_call" | custom-call | flops 30000000 | bytes 2000000 | tf_op jit(solution)/shard_map/pallas_call | solution.py:551
  13.5 0.0 collective-permute-done.3.refs_3_
  13.5 0.0 collective-permute-done.refs_0_
  13.5 0.0 collective-permute-done.1.refs_1_
  13.5 5.7 %shard_map.138 = (f32[9,56,128]{2,1,0:T(8,128)S(1)}, f32[9,56,128]{2,1,0:T(8,128)S(1)}, f32[96,1152]{1,0:T(8,128)S(1)}, bf16[448,512]{1,0:T(8,128)(2,1)S(1)}, f3...) custom-call(f32[112,128]{1,0:T(8,128)S(1)} %collective-permute-done.refs_0_, ...), custom_call_target="tpu_custom_call" | custom-call | flops 70000000 | bytes 2000000 | tf_op jit(solution)/shard_map/pallas_call | solution.py:551
  19.3 0.1 collective-permute-start.6
  19.4 2.9 %collective-permute-start.4 = (f32[112,128]{1,0:T(8,128)S(1)}, f32[112,128]{1,0:T(8,128)S(1)}, u32[]{:S(2)}, u32[]{:S(2)}) collective-permute-start(f32[112,128]{1,0:T(8,128)S(1)} %get-tuple-element.84), channel_id=1, source_target_pairs={{0,4},{1,5},{2,6},{3,7},{4,0},{5,1},{6,2},{7,3},{8,12},{9,13},{10,... | collective-permute-start | bytes 172040 | tf_op jit(solution)/shard_map/ppermute | solution.py:579
  22.3 0.2 collective-permute-start.5
  22.4 0.0 collective-permute-done.6.refs_2_
  22.5 1.5 %collective-permute-start.7 = (f32[16,256]{1,0:T(8,128)S(1)}, f32[16,256]{1,0:T(8,128)S(1)}, u32[]{:S(2)}, u32[]{:S(2)}) collective-permute-start(f32[16,256]{1,0:T(8,128)S(1)} %pad_maximum_fusion.1), channel_id=1, source_target_pairs={{0,2},{1,3},{2,0},{3,1},{4,6},{5,7},{6,4},{7,5},{8,10},{9,11},{10,... | collective-permute-start | bytes 49160 | tf_op jit(solution)/shard_map/ppermute | solution.py:583
  23.9 1.5 %shard_map.139 = (f32[9,56,128]{2,1,0:T(8,128)S(1)}, f32[216,512]{1,0:T(8,128)S(1)}, f32[96,1152]{1,0:T(8,128)S(1)}) custom-call(f32[9,56,128]{2,1,0:T(8,128)S(1)} %get-tuple-element.88.refs_0_, f32[9,56,128]{2,1,0:T(8,128)S(1)} %get-tuple-element.89.refs_1_, f32[328,128]{1,0:T(8,128)S(1)} %get-tuple-element.66.refs_10_.refs_13_.refs_2_, ...), custom_call_target="tpu_custom_call" | custom-call | flops 30000000 | bytes 2000000 | tf_op jit(solution)/shard_map/pallas_call | solution.py:551
  25.4 0.8 %collective-permute-done.7.refs_3_ = f32[16,256]{1,0:T(8,128)S(1)} collective-permute-done((f32[16,256]{1,0:T(8,128)S(1)}, f32[16,256]{1,0:T(8,128)S(1)}, u32[]{:S(2)}, u32[]{:S(2)}) %collective-permute-start.7) | collective-permute-done | bytes 16416 | tf_op jit(solution)/shard_map/ppermute | solution.py:583
  26.3 0.0 collective-permute-done.4.refs_0_
  26.3 0.0 collective-permute-done.5.refs_1_
  26.3 1.8 %shard_map.140 = f32[9,56,128]{2,1,0:T(8,128)} custom-call(f32[112,128]{1,0:T(8,128)S(1)} %collective-permute-done.4.refs_0_, f32[112,128]{1,0:T(8,128)S(1)} %collective-permute-done.5.refs_1_, f32[16,256]{1,0:T(8,128)S(1)} %collective-permute-done.6.refs_2_, f32[16,256]{1,0:T(8,128)S(1)} %collective-permute-done.7.refs_3_, ...), custom_call_target="tpu_custom_call" | custom-call | flops 10000000 | bytes 2000000 | tf_op jit(solution)/shard_map/pallas_call | solution.py:551
  (4 shorter events, 0.0 us)
Async XLA Ops:
  6.4 3.3 %collective-permute-start.2 = (f32[16,256]{1,0:T(8,128)S(1)}, f32[16,256]{1,0:T(8,128)S(1)}, u32[]{:S(2)}, u32[]{:S(2)}) collective-permute-start(f32[16,256]{1,0:T(8,128)S(1)} %get-tuple-element.54), channel_id=1, source_target_pairs={{0,1},{1,0},{2,3},{3,2},{4,5},{5,4},{6,7},{7,6},{8,9},{9,8},{10,11... | collective-permute-start | bytes 49160 | tf_op jit(solution)/shard_map/ppermute | solution.py:577
  6.9 6.6 %collective-permute-start = (f32[112,128]{1,0:T(8,128)S(1)}, f32[112,128]{1,0:T(8,128)S(1)}, u32[]{:S(2)}, u32[]{:S(2)}) collective-permute-start(f32[112,128]{1,0:T(8,128)S(1)} %get-tuple-element.52), channel_id=1, source_target_pairs={{0,4},{1,5},{2,6},{3,7},{4,0},{5,1},{6,2},{7,3},{8,12},{9,13},{10,... | collective-permute-start | bytes 172040 | tf_op jit(solution)/shard_map/ppermute | solution.py:579
  9.5 4.0 %collective-permute-start.1 = (f32[112,128]{1,0:T(8,128)S(1)}, f32[112,128]{1,0:T(8,128)S(1)}, u32[]{:S(2)}, u32[]{:S(2)}) collective-permute-start(f32[112,128]{1,0:T(8,128)S(1)} %get-tuple-element.53), channel_id=1, source_target_pairs={{0,1},{1,0},{2,3},{3,2},{4,8},{5,9},{6,10},{7,11},{8,4},{9,5},{10,... | collective-permute-start | bytes 172040 | tf_op jit(solution)/shard_map/ppermute | solution.py:578
  9.6 3.8 %collective-permute-start.3 = (f32[16,256]{1,0:T(8,128)S(1)}, f32[16,256]{1,0:T(8,128)S(1)}, u32[]{:S(2)}, u32[]{:S(2)}) collective-permute-start(f32[16,256]{1,0:T(8,128)S(1)} %pad_maximum_fusion), channel_id=1, source_target_pairs={{0,2},{1,3},{2,0},{3,1},{4,6},{5,7},{6,4},{7,5},{8,10},{9,11},{10,... | collective-permute-start | bytes 49160 | tf_op jit(solution)/shard_map/ppermute | solution.py:583
  19.3 3.2 %collective-permute-start.6 = (f32[16,256]{1,0:T(8,128)S(1)}, f32[16,256]{1,0:T(8,128)S(1)}, u32[]{:S(2)}, u32[]{:S(2)}) collective-permute-start(f32[16,256]{1,0:T(8,128)S(1)} %get-tuple-element.86), channel_id=1, source_target_pairs={{0,1},{1,0},{2,3},{3,2},{4,5},{5,4},{6,7},{7,6},{8,9},{9,8},{10,11... | collective-permute-start | bytes 49160 | tf_op jit(solution)/shard_map/ppermute | solution.py:577
  19.4 6.9 %collective-permute-start.4 = (f32[112,128]{1,0:T(8,128)S(1)}, f32[112,128]{1,0:T(8,128)S(1)}, u32[]{:S(2)}, u32[]{:S(2)}) collective-permute-start(f32[112,128]{1,0:T(8,128)S(1)} %get-tuple-element.84), channel_id=1, source_target_pairs={{0,4},{1,5},{2,6},{3,7},{4,0},{5,1},{6,2},{7,3},{8,12},{9,13},{10,... | collective-permute-start | bytes 172040 | tf_op jit(solution)/shard_map/ppermute | solution.py:579
  22.3 4.0 %collective-permute-start.5 = (f32[112,128]{1,0:T(8,128)S(1)}, f32[112,128]{1,0:T(8,128)S(1)}, u32[]{:S(2)}, u32[]{:S(2)}) collective-permute-start(f32[112,128]{1,0:T(8,128)S(1)} %get-tuple-element.85), channel_id=1, source_target_pairs={{0,1},{1,0},{2,3},{3,2},{4,8},{5,9},{6,10},{7,11},{8,4},{9,5},{10,... | collective-permute-start | bytes 172040 | tf_op jit(solution)/shard_map/ppermute | solution.py:578
  22.5 3.8 %collective-permute-start.7 = (f32[16,256]{1,0:T(8,128)S(1)}, f32[16,256]{1,0:T(8,128)S(1)}, u32[]{:S(2)}, u32[]{:S(2)}) collective-permute-start(f32[16,256]{1,0:T(8,128)S(1)} %pad_maximum_fusion.1), channel_id=1, source_target_pairs={{0,2},{1,3},{2,0},{3,1},{4,6},{5,7},{6,4},{7,5},{8,10},{9,11},{10,... | collective-permute-start | bytes 49160 | tf_op jit(solution)/shard_map/ppermute | solution.py:583
where the time goes:
time: 28.2 us; the launch traced here: 28 us
  Pallas kernels  17.7 us (63%)
  starting transfers between devices  9.48 us (34%)
  waiting for transfers between devices  0.83 us (3%)
    pallas_call x5, Pallas kernels, call(): pl.pallas_call(functools.partial(fn, sizes), out_shape=outs, in_specs=[pl...  17.7 us
    ppermute x2, starting transfers between devices, trade(): ra = lax.ppermute(pa, combined, even_pairs)  5.48 us
    ppermute x2, starting transfers between devices, trade(): lax.ppermute(jnp.concatenate([part, passed], axis=0), combined, sub_pairs...  3.02 us
    ppermute x2, waiting for transfers between devices, trade(): lax.ppermute(jnp.concatenate([part, passed], axis=0), combined, sub_pairs...  0.82 us
    ppermute x2, starting transfers between devices, trade(): r1 = lax.ppermute(p1, combined, sub_pairs(1))  0.65 us
  transfers between devices with their start and end apart: 8, of which 1 were waited for; matrix products, arithmetic and copies ran while one was open for 0% of the time, Pallas kernels for 14%

commit v1 on v0

--- a/solution.py
+++ b/solution.py
@@ -109,7 +109,7 @@
 def predictor(moved_ref, other_ref, star_ref, left, first_ref, late_ref, sizes, finish):
     def weigh(weights, degree):
         w_half, w_full = weights
-        scale = -1.0 / (degree + 1).astype(F32)
+        scale = -1.0 / (degree + 1)
         return w_half * (scale * HALF), w_full * scale
 
     def emitter(weights):
@@ -130,8 +130,10 @@
         return weights
 
     steps = ORDER - 1
-    weights = lax.fori_loop(0, steps // 2, two, (jnp.float32(HALF), jnp.float32(1.0)))
-    w_half, w_full = weigh(weights, jnp.int32(steps))
+    weights = (HALF, 1.0)
+    for i in range(steps // 2):
+        weights = two(i, weights)
+    w_half, w_full = weigh(weights, steps)
     for g in groups(sizes):
         acc = mix_group(moved_ref, star_ref, sizes, g)
         values = []

time: 28.2 us -> 27.4 us (0.972)
  Pallas kernels: 17.7 us -> 16.9 us
    pallas_call x5, Pallas kernels: 17.7 us -> 16.9 us  [call(): pl.pallas_call(functools.partial(fn, sizes), out_shape=outs, in_specs=[pl...]
where the time goes in v1:
time: 27.4 us; the launch traced here: 27.3 us
  Pallas kernels  16.9 us (62%)
  starting transfers between devices  9.49 us (35%)
  waiting for transfers between devices  0.82 us (3%)
    pallas_call x5, Pallas kernels, call(): pl.pallas_call(functools.partial(fn, sizes), out_shape=outs, in_specs=[pl...  16.9 us
    ppermute x2, starting transfers between devices, trade(): ra = lax.ppermute(pa, combined, even_pairs)  5.47 us
    ppermute x2, starting transfers between devices, trade(): lax.ppermute(jnp.concatenate([part, passed], axis=0), combined, sub_pairs...  3.03 us
    ppermute x2, waiting for transfers between devices, trade(): lax.ppermute(jnp.concatenate([part, passed], axis=0), combined, sub_pairs...  0.8 us
    ppermute x2, starting transfers between devices, trade(): r1 = lax.ppermute(p1, combined, sub_pairs(1))  0.65 us
  transfers between devices with their start and end apart: 8, of which 1 were waited for; matrix products, arithmetic and copies ran while one was open for 0% of the time, Pallas kernels for 14%

profile of v1, /device:TPU:0, one launch (start us, length us, event | category | flops | bytes accessed | tf_op | source)
XLA Modules:
  0.0 27.3 jit_solution(13123664473552396718)
XLA Ops:
  0.0 6.0 %shard_map.136 = (s32[1,128]{1,0:T(1,128)S(1)}, s32[1,128]{1,0:T(1,128)S(1)}, f32[9,9,4,64]{3,2,1,0:T(4,128)S(1)}, f32[9,9,4,64]{3,2,1,0:T(4,128)S(1)}, s32[4,12...) custom-call(f32[9,56,128]{2,1,0:T(8,128)} %bitcast.10, ...), custom_call_target="tpu_custom_call" | custom-call | flops 60000000 | bytes 2000000 | tf_op jit(solution)/shard_map/pallas_call | solution.py:553
  6.0 0.5 %collective-permute-start.2 = (f32[16,256]{1,0:T(8,128)S(1)}, f32[16,256]{1,0:T(8,128)S(1)}, u32[]{:S(2)}, u32[]{:S(2)}) collective-permute-start(f32[16,256]{1,0:T(8,128)S(1)} %get-tuple-element.54), channel_id=1, source_target_pairs={{0,1},{1,0},{2,3},{3,2},{4,5},{5,4},{6,7},{7,6},{8,9},{9,8},{10,11... | collective-permute-start | bytes 49160 | tf_op jit(solution)/shard_map/ppermute | solution.py:579
  6.5 2.6 %collective-permute-start = (f32[112,128]{1,0:T(8,128)S(1)}, f32[112,128]{1,0:T(8,128)S(1)}, u32[]{:S(2)}, u32[]{:S(2)}) collective-permute-start(f32[112,128]{1,0:T(8,128)S(1)} %get-tuple-element.52), channel_id=1, source_target_pairs={{0,4},{1,5},{2,6},{3,7},{4,0},{5,1},{6,2},{7,3},{8,12},{9,13},{10,... | collective-permute-start | bytes 172040 | tf_op jit(solution)/shard_map/ppermute | solution.py:581
  9.1 0.2 collective-permute-start.1
  9.3 0.0 collective-permute-done.2.refs_2_
  9.3 1.5 %collective-permute-start.3 = (f32[16,256]{1,0:T(8,128)S(1)}, f32[16,256]{1,0:T(8,128)S(1)}, u32[]{:S(2)}, u32[]{:S(2)}) collective-permute-start(f32[16,256]{1,0:T(8,128)S(1)} %pad_maximum_fusion), channel_id=1, source_target_pairs={{0,2},{1,3},{2,0},{3,1},{4,6},{5,7},{6,4},{7,5},{8,10},{9,11},{10,... | collective-permute-start | bytes 49160 | tf_op jit(solution)/shard_map/ppermute | solution.py:585
  10.9 2.3 %shard_map.137 = (f32[9,56,128]{2,1,0:T(8,128)S(1)}, f32[216,512]{1,0:T(8,128)S(1)}, f32[96,1152]{1,0:T(8,128)S(1)}, f32[328,128]{1,0:T(8,128)S(1)}, f32[328,128...) custom-call(s32[1,128]{1,0:T(1,128)S(1)} %get-tuple-element.56.refs_, ...), custom_call_target="tpu_custom_call" | custom-call | flops 30000000 | bytes 2000000 | tf_op jit(solution)/shard_map/pallas_call | solution.py:553
  13.1 0.0 collective-permute-done.3.refs_3_
  13.1 0.0 collective-permute-done.refs_0_
  13.2 0.0 collective-permute-done.1.refs_1_
  13.2 5.3 %shard_map.138 = (f32[9,56,128]{2,1,0:T(8,128)S(1)}, f32[9,56,128]{2,1,0:T(8,128)S(1)}, f32[96,1152]{1,0:T(8,128)S(1)}, bf16[448,512]{1,0:T(8,128)(2,1)S(1)}, f3...) custom-call(f32[112,128]{1,0:T(8,128)S(1)} %collective-permute-done.refs_0_, ...), custom_call_target="tpu_custom_call" | custom-call | flops 70000000 | bytes 2000000 | tf_op jit(solution)/shard_map/pallas_call | solution.py:553
  18.5 0.1 collective-permute-start.6
  18.6 2.9 %collective-permute-start.4 = (f32[112,128]{1,0:T(8,128)S(1)}, f32[112,128]{1,0:T(8,128)S(1)}, u32[]{:S(2)}, u32[]{:S(2)}) collective-permute-start(f32[112,128]{1,0:T(8,128)S(1)} %get-tuple-element.84), channel_id=1, source_target_pairs={{0,4},{1,5},{2,6},{3,7},{4,0},{5,1},{6,2},{7,3},{8,12},{9,13},{10,... | collective-permute-start | bytes 172040 | tf_op jit(solution)/shard_map/ppermute | solution.py:581
  21.5 0.2 collective-permute-start.5
  21.7 0.0 collective-permute-done.6.refs_2_
  21.7 1.5 %collective-permute-start.7 = (f32[16,256]{1,0:T(8,128)S(1)}, f32[16,256]{1,0:T(8,128)S(1)}, u32[]{:S(2)}, u32[]{:S(2)}) collective-permute-start(f32[16,256]{1,0:T(8,128)S(1)} %pad_maximum_fusion.1), channel_id=1, source_target_pairs={{0,2},{1,3},{2,0},{3,1},{4,6},{5,7},{6,4},{7,5},{8,10},{9,11},{10,... | collective-permute-start | bytes 49160 | tf_op jit(solution)/shard_map/ppermute | solution.py:585
  23.2 1.5 %shard_map.139 = (f32[9,56,128]{2,1,0:T(8,128)S(1)}, f32[216,512]{1,0:T(8,128)S(1)}, f32[96,1152]{1,0:T(8,128)S(1)}) custom-call(f32[9,56,128]{2,1,0:T(8,128)S(1)} %get-tuple-element.88.refs_0_, f32[9,56,128]{2,1,0:T(8,128)S(1)} %get-tuple-element.89.refs_1_, f32[328,128]{1,0:T(8,128)S(1)} %get-tuple-element.66.refs_10_.refs_13_.refs_2_, ...), custom_call_target="tpu_custom_call" | custom-call | flops 30000000 | bytes 2000000 | tf_op jit(solution)/shard_map/pallas_call | solution.py:553
  24.7 0.8 %collective-permute-done.7.refs_3_ = f32[16,256]{1,0:T(8,128)S(1)} collective-permute-done((f32[16,256]{1,0:T(8,128)S(1)}, f32[16,256]{1,0:T(8,128)S(1)}, u32[]{:S(2)}, u32[]{:S(2)}) %collective-permute-start.7) | collective-permute-done | bytes 16416 | tf_op jit(solution)/shard_map/ppermute | solution.py:585
  25.5 0.0 collective-permute-done.4.refs_0_
  25.5 0.0 collective-permute-done.5.refs_1_
  25.5 1.8 %shard_map.140 = f32[9,56,128]{2,1,0:T(8,128)} custom-call(f32[112,128]{1,0:T(8,128)S(1)} %collective-permute-done.4.refs_0_, f32[112,128]{1,0:T(8,128)S(1)} %collective-permute-done.5.refs_1_, f32[16,256]{1,0:T(8,128)S(1)} %collective-permute-done.6.refs_2_, f32[16,256]{1,0:T(8,128)S(1)} %collective-permute-done.7.refs_3_, ...), custom_call_target="tpu_custom_call" | custom-call | flops 10000000 | bytes 2000000 | tf_op jit(solution)/shard_map/pallas_call | solution.py:553
  (4 shorter events, 0.0 us)
Async XLA Ops:
  6.0 3.3 %collective-permute-start.2 = (f32[16,256]{1,0:T(8,128)S(1)}, f32[16,256]{1,0:T(8,128)S(1)}, u32[]{:S(2)}, u32[]{:S(2)}) collective-permute-start(f32[16,256]{1,0:T(8,128)S(1)} %get-tuple-element.54), channel_id=1, source_target_pairs={{0,1},{1,0},{2,3},{3,2},{4,5},{5,4},{6,7},{7,6},{8,9},{9,8},{10,11... | collective-permute-start | bytes 49160 | tf_op jit(solution)/shard_map/ppermute | solution.py:579
  6.5 6.6 %collective-permute-start = (f32[112,128]{1,0:T(8,128)S(1)}, f32[112,128]{1,0:T(8,128)S(1)}, u32[]{:S(2)}, u32[]{:S(2)}) collective-permute-start(f32[112,128]{1,0:T(8,128)S(1)} %get-tuple-element.52), channel_id=1, source_target_pairs={{0,4},{1,5},{2,6},{3,7},{4,0},{5,1},{6,2},{7,3},{8,12},{9,13},{10,... | collective-permute-start | bytes 172040 | tf_op jit(solution)/shard_map/ppermute | solution.py:581
  9.1 4.0 %collective-permute-start.1 = (f32[112,128]{1,0:T(8,128)S(1)}, f32[112,128]{1,0:T(8,128)S(1)}, u32[]{:S(2)}, u32[]{:S(2)}) collective-permute-start(f32[112,128]{1,0:T(8,128)S(1)} %get-tuple-element.53), channel_id=1, source_target_pairs={{0,1},{1,0},{2,3},{3,2},{4,8},{5,9},{6,10},{7,11},{8,4},{9,5},{10,... | collective-permute-start | bytes 172040 | tf_op jit(solution)/shard_map/ppermute | solution.py:580
  9.3 3.8 %collective-permute-start.3 = (f32[16,256]{1,0:T(8,128)S(1)}, f32[16,256]{1,0:T(8,128)S(1)}, u32[]{:S(2)}, u32[]{:S(2)}) collective-permute-start(f32[16,256]{1,0:T(8,128)S(1)} %pad_maximum_fusion), channel_id=1, source_target_pairs={{0,2},{1,3},{2,0},{3,1},{4,6},{5,7},{6,4},{7,5},{8,10},{9,11},{10,... | collective-permute-start | bytes 49160 | tf_op jit(solution)/shard_map/ppermute | solution.py:585
  18.5 3.2 %collective-permute-start.6 = (f32[16,256]{1,0:T(8,128)S(1)}, f32[16,256]{1,0:T(8,128)S(1)}, u32[]{:S(2)}, u32[]{:S(2)}) collective-permute-start(f32[16,256]{1,0:T(8,128)S(1)} %get-tuple-element.86), channel_id=1, source_target_pairs={{0,1},{1,0},{2,3},{3,2},{4,5},{5,4},{6,7},{7,6},{8,9},{9,8},{10,11... | collective-permute-start | bytes 49160 | tf_op jit(solution)/shard_map/ppermute | solution.py:579
  18.6 6.9 %collective-permute-start.4 = (f32[112,128]{1,0:T(8,128)S(1)}, f32[112,128]{1,0:T(8,128)S(1)}, u32[]{:S(2)}, u32[]{:S(2)}) collective-permute-start(f32[112,128]{1,0:T(8,128)S(1)} %get-tuple-element.84), channel_id=1, source_target_pairs={{0,4},{1,5},{2,6},{3,7},{4,0},{5,1},{6,2},{7,3},{8,12},{9,13},{10,... | collective-permute-start | bytes 172040 | tf_op jit(solution)/shard_map/ppermute | solution.py:581
  21.5 4.0 %collective-permute-start.5 = (f32[112,128]{1,0:T(8,128)S(1)}, f32[112,128]{1,0:T(8,128)S(1)}, u32[]{:S(2)}, u32[]{:S(2)}) collective-permute-start(f32[112,128]{1,0:T(8,128)S(1)} %get-tuple-element.85), channel_id=1, source_target_pairs={{0,1},{1,0},{2,3},{3,2},{4,8},{5,9},{6,10},{7,11},{8,4},{9,5},{10,... | collective-permute-start | bytes 172040 | tf_op jit(solution)/shard_map/ppermute | solution.py:580
  21.7 3.8 %collective-permute-start.7 = (f32[16,256]{1,0:T(8,128)S(1)}, f32[16,256]{1,0:T(8,128)S(1)}, u32[]{:S(2)}, u32[]{:S(2)}) collective-permute-start(f32[16,256]{1,0:T(8,128)S(1)} %pad_maximum_fusion.1), channel_id=1, source_target_pairs={{0,2},{1,3},{2,0},{3,1},{4,6},{5,7},{6,4},{7,5},{8,10},{9,11},{10,... | collective-permute-start | bytes 49160 | tf_op jit(solution)/shard_map/ppermute | solution.py:585

commit v2 on v1

--- a/solution.py
+++ b/solution.py
@@ -98,15 +98,22 @@
     return slice(g * GROUP * 128, (g + 1) * GROUP * 128)
 
 
-def advance(src_ref, dst_ref, star_ref, left, sizes, emit):
+def advance(src_ref, dst_ref, star_ref, left, sizes, emit, between):
     for g in groups(sizes):
         acc = mix_group(src_ref, star_ref, sizes, g)
         for i in range(GROUP):
             emit(g * GROUP + i, acc[i])
         dst_ref[:, group_lanes(g)] = dot(left, stack_right(acc))[: dst_ref.shape[0]]
-
-
-def predictor(moved_ref, other_ref, star_ref, left, first_ref, late_ref, sizes, finish):
+        between()
+
+
+def predictor(moved_ref, other_ref, star_ref, left, first_ref, late_ref, sizes, finish, extra=()):
+    extra = list(extra)
+
+    def between():
+        if extra:
+            extra.pop(0)()
+
     def weigh(weights, degree):
         w_half, w_full = weights
         scale = -1.0 / (degree + 1)
@@ -124,9 +131,9 @@
 
     def two(i, weights):
         weights = weigh(weights, 2 * i + 1)
-        advance(moved_ref, other_ref, star_ref, left, sizes, emitter(weights))
+        advance(moved_ref, other_ref, star_ref, left, sizes, emitter(weights), between)
         weights = weigh(weights, 2 * i + 2)
-        advance(other_ref, moved_ref, star_ref, left, sizes, emitter(weights))
+        advance(other_ref, moved_ref, star_ref, left, sizes, emitter(weights), between)
         return weights
 
     steps = ORDER - 1
@@ -288,20 +295,26 @@
         for i in range(GROUP):
             first_ref[g * GROUP + i] = values[i] * HALF
             late_ref[g * GROUP + i] = values[i] * (1.0 - HALF)
-    copies[4].wait()
-    picks_of_sends(send_ref, pick_ref, pick_sub_ref)
-    copies[5].wait()
-    faces, face_basis = 4, restrict_ref.shape[0]
-    rstage_ref[...] = jnp.zeros_like(rstage_ref)
-    for f in range(faces):
-        rstage_ref[f * PAD : f * PAD + face_basis, :basis] = restrict_ref[:, f, :]
-    rleft_ref[...] = stack_left(rstage_ref[:, :basis])
+    for copy in copies[4:6]:
+        copy.wait()
+    def send_picks():
+        picks_of_sends(send_ref, pick_ref, pick_sub_ref)
+
+    def restrict_left():
+        rstage_ref[...] = jnp.zeros_like(rstage_ref)
+        for f in range(4):
+            rstage_ref[f * PAD : f * PAD + restrict_ref.shape[0], :basis] = restrict_ref[:, f, :]
+        rleft_ref[...] = stack_left(rstage_ref[:, :basis])
+
+    send_picks()
+    restrict_left()
 
     def finish(p, first):
         first_ref[p] = first
         return first
 
-    for g, values in predictor(moved_ref, other_ref, star_ref, left, first_ref, late_ref, sizes, finish):
+    for g, values in predictor(moved_ref, other_ref, star_ref, left, first_ref, late_ref, sizes, finish,
+                               []):
         project(g, values, rleft_ref[...], proj_ref)
     by_face(proj_ref, faces_ref, sizes)
     payloads(faces_ref, pick_ref, pick_sub_ref, slot_ref, (pa_ref, pb_ref, p1_ref, pk_refs), sizes)
@@ -476,12 +489,18 @@
     ra_ref, rb_ref, r1_ref, *refs = refs
     rk_refs, refs = refs[:xs], refs[xs:]
     (oleft_ref, ghost_turn_ref, ghost_pick_ref, gath_ref, comb_ref, plus_ref, lleft_ref, llow_ref, partial_ref,
-     out_ref, slot_ref, ghost_ref, gsum_ref) = refs
+     out_hbm, slot_ref, ghost_ref, gsum_ref, out_ref, sems) = refs
+    copies = []
     for g, values in neighbour_part((ra_ref, rb_ref, r1_ref, rk_refs), oleft_ref, ghost_turn_ref, ghost_pick_ref,
                                     gath_ref, comb_ref, plus_ref, lleft_ref, llow_ref, partial_ref, slot_ref,
                                     ghost_ref, gsum_ref, sizes):
         for i in range(GROUP):
             out_ref[g * GROUP + i] = values[i]
+        part = pl.ds(g * GROUP, GROUP)
+        copies.append(pltpu.make_async_copy(out_ref.at[part], out_hbm.at[part], sems.at[g]))
+        copies[-1].start()
+    for copy in copies:
+        copy.wait()
 
 
 def body(
@@ -546,8 +565,8 @@
     pslot_s = pltpu.VMEM((ghosts - 2 * CAP_DOM, sub_lanes), F32)
     ghost_s = pltpu.VMEM((2 * rows, 256), BF16)
 
-    def call(fn, outs, scratches, operands, flops, space=pltpu.VMEM):
-        vmem = pl.BlockSpec(memory_space=pltpu.VMEM)
+    def call(fn, outs, scratches, operands, flops, space=pltpu.VMEM, out_space=pltpu.VMEM):
+        vmem = pl.BlockSpec(memory_space=out_space)
         if space is pltpu.HBM:
             operands = [pltpu.with_memory_space_constraint(x, pltpu.HBM) for x in operands]
         return pl.pallas_call(
@@ -635,9 +654,10 @@
     result = call(
         kernel_last,
         whole,
-        [slot_s, ghost_s, scratch(gath_t)],
+        [slot_s, ghost_s, scratch(gath_t), scratch(whole), pltpu.SemaphoreType.DMA((variables // GROUP,))],
         received + common + [gath, comb, plus, lleft, llow, partial],
         10_000_000,
+        out_space=pltpu.HBM,
     )
     return jnp.transpose(result, (1, 0, 2))
 

time: 27.4 us -> 27.3 us (level)
  no operation moved by 1% of the time
where the time goes in v2:
time: 27.3 us; the launch traced here: 27.1 us
  Pallas kernels  16.8 us (62%)
  starting transfers between devices  9.47 us (35%)
  waiting for transfers between devices  0.83 us (3%)
    pallas_call x5, Pallas kernels, call(): pl.pallas_call(functools.partial(fn, sizes), out_shape=outs, in_specs=[pl...  16.8 us
    ppermute x2, starting transfers between devices, trade(): ra = lax.ppermute(pa, combined, even_pairs)  5.47 us
    ppermute x2, starting transfers between devices, trade(): lax.ppermute(jnp.concatenate([part, passed], axis=0), combined, sub_pairs...  3.03 us
    ppermute x2, waiting for transfers between devices, trade(): lax.ppermute(jnp.concatenate([part, passed], axis=0), combined, sub_pairs...  0.82 us
    ppermute x2, starting transfers between devices, trade(): r1 = lax.ppermute(p1, combined, sub_pairs(1))  0.63 us
  transfers between devices with their start and end apart: 8, of which 1 were waited for; matrix products, arithmetic and copies ran while one was open for 0% of the time, Pallas kernels for 14%

profile of v2, /device:TPU:0, one launch (start us, length us, event | category | flops | bytes accessed | tf_op | source)
XLA Modules:
  0.0 27.1 jit_solution(8232022078191067768)
XLA Ops:
  0.0 5.9 %shard_map.136 = (s32[1,128]{1,0:T(1,128)S(1)}, s32[1,128]{1,0:T(1,128)S(1)}, f32[9,9,4,64]{3,2,1,0:T(4,128)S(1)}, f32[9,9,4,64]{3,2,1,0:T(4,128)S(1)}, s32[4,12...) custom-call(f32[9,56,128]{2,1,0:T(8,128)} %bitcast.10, ...), custom_call_target="tpu_custom_call" | custom-call | flops 60000000 | bytes 2000000 | tf_op jit(solution)/shard_map/pallas_call | solution.py:572
  5.9 0.5 %collective-permute-start.2 = (f32[16,256]{1,0:T(8,128)S(1)}, f32[16,256]{1,0:T(8,128)S(1)}, u32[]{:S(2)}, u32[]{:S(2)}) collective-permute-start(f32[16,256]{1,0:T(8,128)S(1)} %get-tuple-element.54), channel_id=1, source_target_pairs={{0,1},{1,0},{2,3},{3,2},{4,5},{5,4},{6,7},{7,6},{8,9},{9,8},{10,11... | collective-permute-start | bytes 49160 | tf_op jit(solution)/shard_map/ppermute | solution.py:598
  6.4 2.6 %collective-permute-start = (f32[112,128]{1,0:T(8,128)S(1)}, f32[112,128]{1,0:T(8,128)S(1)}, u32[]{:S(2)}, u32[]{:S(2)}) collective-permute-start(f32[112,128]{1,0:T(8,128)S(1)} %get-tuple-element.52), channel_id=1, source_target_pairs={{0,4},{1,5},{2,6},{3,7},{4,0},{5,1},{6,2},{7,3},{8,12},{9,13},{10,... | collective-permute-start | bytes 172040 | tf_op jit(solution)/shard_map/ppermute | solution.py:600
  9.0 0.2 collective-permute-start.1
  9.2 0.0 collective-permute-done.2.refs_2_
  9.2 1.6 %collective-permute-start.3 = (f32[16,256]{1,0:T(8,128)S(1)}, f32[16,256]{1,0:T(8,128)S(1)}, u32[]{:S(2)}, u32[]{:S(2)}) collective-permute-start(f32[16,256]{1,0:T(8,128)S(1)} %pad_maximum_fusion), channel_id=1, source_target_pairs={{0,2},{1,3},{2,0},{3,1},{4,6},{5,7},{6,4},{7,5},{8,10},{9,11},{10,... | collective-permute-start | bytes 49160 | tf_op jit(solution)/shard_map/ppermute | solution.py:604
  10.8 2.3 %shard_map.137 = (f32[9,56,128]{2,1,0:T(8,128)S(1)}, f32[216,512]{1,0:T(8,128)S(1)}, f32[96,1152]{1,0:T(8,128)S(1)}, f32[328,128]{1,0:T(8,128)S(1)}, f32[328,128...) custom-call(s32[1,128]{1,0:T(1,128)S(1)} %get-tuple-element.56.refs_, ...), custom_call_target="tpu_custom_call" | custom-call | flops 30000000 | bytes 2000000 | tf_op jit(solution)/shard_map/pallas_call | solution.py:572
  13.1 0.0 collective-permute-done.3.refs_3_
  13.1 0.0 collective-permute-done.refs_0_
  13.1 0.0 collective-permute-done.1.refs_1_
  13.1 5.3 %shard_map.138 = (f32[9,56,128]{2,1,0:T(8,128)S(1)}, f32[9,56,128]{2,1,0:T(8,128)S(1)}, f32[96,1152]{1,0:T(8,128)S(1)}, bf16[448,512]{1,0:T(8,128)(2,1)S(1)}, f3...) custom-call(f32[112,128]{1,0:T(8,128)S(1)} %collective-permute-done.refs_0_, ...), custom_call_target="tpu_custom_call" | custom-call | flops 70000000 | bytes 2000000 | tf_op jit(solution)/shard_map/pallas_call | solution.py:572
  18.4 0.1 collective-permute-start.6
  18.5 2.9 %collective-permute-start.4 = (f32[112,128]{1,0:T(8,128)S(1)}, f32[112,128]{1,0:T(8,128)S(1)}, u32[]{:S(2)}, u32[]{:S(2)}) collective-permute-start(f32[112,128]{1,0:T(8,128)S(1)} %get-tuple-element.84), channel_id=1, source_target_pairs={{0,4},{1,5},{2,6},{3,7},{4,0},{5,1},{6,2},{7,3},{8,12},{9,13},{10,... | collective-permute-start | bytes 172040 | tf_op jit(solution)/shard_map/ppermute | solution.py:600
  21.4 0.2 collective-permute-start.5
  21.6 0.0 collective-permute-done.6.refs_2_
  21.6 1.5 %collective-permute-start.7 = (f32[16,256]{1,0:T(8,128)S(1)}, f32[16,256]{1,0:T(8,128)S(1)}, u32[]{:S(2)}, u32[]{:S(2)}) collective-permute-start(f32[16,256]{1,0:T(8,128)S(1)} %pad_maximum_fusion.1), channel_id=1, source_target_pairs={{0,2},{1,3},{2,0},{3,1},{4,6},{5,7},{6,4},{7,5},{8,10},{9,11},{10,... | collective-permute-start | bytes 49160 | tf_op jit(solution)/shard_map/ppermute | solution.py:604
  23.1 1.5 %shard_map.139 = (f32[9,56,128]{2,1,0:T(8,128)S(1)}, f32[216,512]{1,0:T(8,128)S(1)}, f32[96,1152]{1,0:T(8,128)S(1)}) custom-call(f32[9,56,128]{2,1,0:T(8,128)S(1)} %get-tuple-element.88.refs_0_, f32[9,56,128]{2,1,0:T(8,128)S(1)} %get-tuple-element.89.refs_1_, f32[328,128]{1,0:T(8,128)S(1)} %get-tuple-element.66.refs_10_.refs_13_.refs_2_, ...), custom_call_target="tpu_custom_call" | custom-call | flops 30000000 | bytes 2000000 | tf_op jit(solution)/shard_map/pallas_call | solution.py:572
  24.6 0.8 %collective-permute-done.7.refs_3_ = f32[16,256]{1,0:T(8,128)S(1)} collective-permute-done((f32[16,256]{1,0:T(8,128)S(1)}, f32[16,256]{1,0:T(8,128)S(1)}, u32[]{:S(2)}, u32[]{:S(2)}) %collective-permute-start.7) | collective-permute-done | bytes 16416 | tf_op jit(solution)/shard_map/ppermute | solution.py:604
  25.4 0.0 collective-permute-done.4.refs_0_
  25.4 0.0 collective-permute-done.5.refs_1_
  25.4 1.7 %shard_map.140 = f32[9,56,128]{2,1,0:T(8,128)} custom-call(f32[112,128]{1,0:T(8,128)S(1)} %collective-permute-done.4.refs_0_, f32[112,128]{1,0:T(8,128)S(1)} %collective-permute-done.5.refs_1_, f32[16,256]{1,0:T(8,128)S(1)} %collective-permute-done.6.refs_2_, f32[16,256]{1,0:T(8,128)S(1)} %collective-permute-done.7.refs_3_, ...), custom_call_target="tpu_custom_call" | custom-call | flops 10000000 | bytes 2000000 | tf_op jit(solution)/shard_map/pallas_call | solution.py:572
  (4 shorter events, 0.0 us)
Async XLA Ops:
  5.9 3.3 %collective-permute-start.2 = (f32[16,256]{1,0:T(8,128)S(1)}, f32[16,256]{1,0:T(8,128)S(1)}, u32[]{:S(2)}, u32[]{:S(2)}) collective-permute-start(f32[16,256]{1,0:T(8,128)S(1)} %get-tuple-element.54), channel_id=1, source_target_pairs={{0,1},{1,0},{2,3},{3,2},{4,5},{5,4},{6,7},{7,6},{8,9},{9,8},{10,11... | collective-permute-start | bytes 49160 | tf_op jit(solution)/shard_map/ppermute | solution.py:598
  6.4 6.6 %collective-permute-start = (f32[112,128]{1,0:T(8,128)S(1)}, f32[112,128]{1,0:T(8,128)S(1)}, u32[]{:S(2)}, u32[]{:S(2)}) collective-permute-start(f32[112,128]{1,0:T(8,128)S(1)} %get-tuple-element.52), channel_id=1, source_target_pairs={{0,4},{1,5},{2,6},{3,7},{4,0},{5,1},{6,2},{7,3},{8,12},{9,13},{10,... | collective-permute-start | bytes 172040 | tf_op jit(solution)/shard_map/ppermute | solution.py:600
  9.0 4.0 %collective-permute-start.1 = (f32[112,128]{1,0:T(8,128)S(1)}, f32[112,128]{1,0:T(8,128)S(1)}, u32[]{:S(2)}, u32[]{:S(2)}) collective-permute-start(f32[112,128]{1,0:T(8,128)S(1)} %get-tuple-element.53), channel_id=1, source_target_pairs={{0,1},{1,0},{2,3},{3,2},{4,8},{5,9},{6,10},{7,11},{8,4},{9,5},{10,... | collective-permute-start | bytes 172040 | tf_op jit(solution)/shard_map/ppermute | solution.py:599
  9.2 3.8 %collective-permute-start.3 = (f32[16,256]{1,0:T(8,128)S(1)}, f32[16,256]{1,0:T(8,128)S(1)}, u32[]{:S(2)}, u32[]{:S(2)}) collective-permute-start(f32[16,256]{1,0:T(8,128)S(1)} %pad_maximum_fusion), channel_id=1, source_target_pairs={{0,2},{1,3},{2,0},{3,1},{4,6},{5,7},{6,4},{7,5},{8,10},{9,11},{10,... | collective-permute-start | bytes 49160 | tf_op jit(solution)/shard_map/ppermute | solution.py:604
  18.4 3.2 %collective-permute-start.6 = (f32[16,256]{1,0:T(8,128)S(1)}, f32[16,256]{1,0:T(8,128)S(1)}, u32[]{:S(2)}, u32[]{:S(2)}) collective-permute-start(f32[16,256]{1,0:T(8,128)S(1)} %get-tuple-element.86), channel_id=1, source_target_pairs={{0,1},{1,0},{2,3},{3,2},{4,5},{5,4},{6,7},{7,6},{8,9},{9,8},{10,11... | collective-permute-start | bytes 49160 | tf_op jit(solution)/shard_map/ppermute | solution.py:598
  18.5 6.9 %collective-permute-start.4 = (f32[112,128]{1,0:T(8,128)S(1)}, f32[112,128]{1,0:T(8,128)S(1)}, u32[]{:S(2)}, u32[]{:S(2)}) collective-permute-start(f32[112,128]{1,0:T(8,128)S(1)} %get-tuple-element.84), channel_id=1, source_target_pairs={{0,4},{1,5},{2,6},{3,7},{4,0},{5,1},{6,2},{7,3},{8,12},{9,13},{10,... | collective-permute-start | bytes 172040 | tf_op jit(solution)/shard_map/ppermute | solution.py:600
  21.4 4.0 %collective-permute-start.5 = (f32[112,128]{1,0:T(8,128)S(1)}, f32[112,128]{1,0:T(8,128)S(1)}, u32[]{:S(2)}, u32[]{:S(2)}) collective-permute-start(f32[112,128]{1,0:T(8,128)S(1)} %get-tuple-element.85), channel_id=1, source_target_pairs={{0,1},{1,0},{2,3},{3,2},{4,8},{5,9},{6,10},{7,11},{8,4},{9,5},{10,... | collective-permute-start | bytes 172040 | tf_op jit(solution)/shard_map/ppermute | solution.py:599
  21.6 3.8 %collective-permute-start.7 = (f32[16,256]{1,0:T(8,128)S(1)}, f32[16,256]{1,0:T(8,128)S(1)}, u32[]{:S(2)}, u32[]{:S(2)}) collective-permute-start(f32[16,256]{1,0:T(8,128)S(1)} %pad_maximum_fusion.1), channel_id=1, source_target_pairs={{0,2},{1,3},{2,0},{3,1},{4,6},{5,7},{6,4},{7,5},{8,10},{9,11},{10,... | collective-permute-start | bytes 49160 | tf_op jit(solution)/shard_map/ppermute | solution.py:604

commit v3 on v2

--- a/solution.py
+++ b/solution.py
@@ -238,10 +238,15 @@
 
 
 def turn_blocks(values, left, turns):
-    out = []
+    stacks = []
     for value in values:
         high, low = split(pad_to(value, OSEC, value.shape[1]))
-        turned = dot(left, jnp.concatenate([high, low, high], axis=0))
+        stacks.append(jnp.concatenate([high, low, high], axis=0))
+    width = values[0].shape[1]
+    whole = dot(left, jnp.concatenate(stacks, axis=1))
+    out = []
+    for q in range(len(values)):
+        turned = whole[:, q * width : (q + 1) * width]
         out.append(
             jnp.where(
                 turns == 0,
@@ -426,8 +431,8 @@
     both = dot(ghost_ref[...], ghost_pick_ref[...])
     used = variables * PAD
     gsum_ref[...] = gath_ref[...] + (both[0:used] + both[rows : rows + used])
+    highs, stacks = [], []
     for g in groups(sizes):
-        highs, stacks = [], []
         faces = [[], [], []]
         for f in range(4):
             frows = slice(f * PAD, (f + 1) * PAD)
@@ -446,11 +451,12 @@
             high, low = split(jnp.concatenate(faces[i], axis=0))
             highs.append(high)
             stacks.append(jnp.concatenate([high, low], axis=0))
-        lifted = dot(lleft_ref[:, : 8 * PAD], jnp.concatenate(stacks, axis=1)) + dot(
-            llow_ref[:, : 4 * PAD], jnp.concatenate(highs, axis=1)
-        )
+    lifted = dot(lleft_ref[:, : 8 * PAD], jnp.concatenate(stacks, axis=1)) + dot(
+        llow_ref[:, : 4 * PAD], jnp.concatenate(highs, axis=1)
+    )
+    for g in groups(sizes):
         yield g, [
-            partial_ref[g * GROUP + i] + lifted[:basis, i * 128 : (i + 1) * 128] for i in range(GROUP)
+            partial_ref[p] + lifted[:basis, p * 128 : (p + 1) * 128] for p in range(g * GROUP, (g + 1) * GROUP)
         ]
 
 

time: 27.3 us -> 27.2 us (level)
  no operation moved by 1% of the time
where the time goes in v3:
time: 27.2 us; the launch traced here: 27 us
  Pallas kernels  16.7 us (61%)
  starting transfers between devices  9.48 us (35%)
  waiting for transfers between devices  0.83 us (3%)
    pallas_call x5, Pallas kernels, call(): pl.pallas_call(functools.partial(fn, sizes), out_shape=outs, in_specs=[pl...  16.7 us
    ppermute x2, starting transfers between devices, trade(): ra = lax.ppermute(pa, combined, even_pairs)  5.47 us
    ppermute x2, starting transfers between devices, trade(): lax.ppermute(jnp.concatenate([part, passed], axis=0), combined, sub_pairs...  3.03 us
    ppermute x2, waiting for transfers between devices, trade(): lax.ppermute(jnp.concatenate([part, passed], axis=0), combined, sub_pairs...  0.81 us
    ppermute x2, starting transfers between devices, trade(): r1 = lax.ppermute(p1, combined, sub_pairs(1))  0.65 us
  transfers between devices with their start and end apart: 8, of which 1 were waited for; matrix products, arithmetic and copies ran while one was open for 0% of the time, Pallas kernels for 14%

profile of v3, /device:TPU:0, one launch (start us, length us, event | category | flops | bytes accessed | tf_op | source)
XLA Modules:
  0.0 27.0 jit_solution(16774316581053768325)
XLA Ops:
  0.0 5.9 %shard_map.136 = (s32[1,128]{1,0:T(1,128)S(1)}, s32[1,128]{1,0:T(1,128)S(1)}, f32[9,9,4,64]{3,2,1,0:T(4,128)S(1)}, f32[9,9,4,64]{3,2,1,0:T(4,128)S(1)}, s32[4,12...) custom-call(f32[9,56,128]{2,1,0:T(8,128)} %bitcast.10, ...), custom_call_target="tpu_custom_call" | custom-call | flops 60000000 | bytes 2000000 | tf_op jit(solution)/shard_map/pallas_call | solution.py:578
  5.9 0.5 %collective-permute-start.2 = (f32[16,256]{1,0:T(8,128)S(1)}, f32[16,256]{1,0:T(8,128)S(1)}, u32[]{:S(2)}, u32[]{:S(2)}) collective-permute-start(f32[16,256]{1,0:T(8,128)S(1)} %get-tuple-element.54), channel_id=1, source_target_pairs={{0,1},{1,0},{2,3},{3,2},{4,5},{5,4},{6,7},{7,6},{8,9},{9,8},{10,11... | collective-permute-start | bytes 49160 | tf_op jit(solution)/shard_map/ppermute | solution.py:604
  6.4 2.6 %collective-permute-start = (f32[112,128]{1,0:T(8,128)S(1)}, f32[112,128]{1,0:T(8,128)S(1)}, u32[]{:S(2)}, u32[]{:S(2)}) collective-permute-start(f32[112,128]{1,0:T(8,128)S(1)} %get-tuple-element.52), channel_id=1, source_target_pairs={{0,4},{1,5},{2,6},{3,7},{4,0},{5,1},{6,2},{7,3},{8,12},{9,13},{10,... | collective-permute-start | bytes 172040 | tf_op jit(solution)/shard_map/ppermute | solution.py:606
  9.0 0.2 collective-permute-start.1
  9.2 0.0 collective-permute-done.2.refs_2_
  9.2 1.6 %collective-permute-start.3 = (f32[16,256]{1,0:T(8,128)S(1)}, f32[16,256]{1,0:T(8,128)S(1)}, u32[]{:S(2)}, u32[]{:S(2)}) collective-permute-start(f32[16,256]{1,0:T(8,128)S(1)} %pad_maximum_fusion), channel_id=1, source_target_pairs={{0,2},{1,3},{2,0},{3,1},{4,6},{5,7},{6,4},{7,5},{8,10},{9,11},{10,... | collective-permute-start | bytes 49160 | tf_op jit(solution)/shard_map/ppermute | solution.py:610
  10.8 2.3 %shard_map.137 = (f32[9,56,128]{2,1,0:T(8,128)S(1)}, f32[216,512]{1,0:T(8,128)S(1)}, f32[96,1152]{1,0:T(8,128)S(1)}, f32[328,128]{1,0:T(8,128)S(1)}, f32[328,128...) custom-call(s32[1,128]{1,0:T(1,128)S(1)} %get-tuple-element.56.refs_, ...), custom_call_target="tpu_custom_call" | custom-call | flops 30000000 | bytes 2000000 | tf_op jit(solution)/shard_map/pallas_call | solution.py:578
  13.1 0.0 collective-permute-done.3.refs_3_
  13.1 0.0 collective-permute-done.refs_0_
  13.1 0.0 collective-permute-done.1.refs_1_
  13.1 5.2 %shard_map.138 = (f32[9,56,128]{2,1,0:T(8,128)S(1)}, f32[9,56,128]{2,1,0:T(8,128)S(1)}, f32[96,1152]{1,0:T(8,128)S(1)}, bf16[448,512]{1,0:T(8,128)(2,1)S(1)}, f3...) custom-call(f32[112,128]{1,0:T(8,128)S(1)} %collective-permute-done.refs_0_, ...), custom_call_target="tpu_custom_call" | custom-call | flops 70000000 | bytes 2000000 | tf_op jit(solution)/shard_map/pallas_call | solution.py:578
  18.3 0.1 collective-permute-start.6
  18.5 2.9 %collective-permute-start.4 = (f32[112,128]{1,0:T(8,128)S(1)}, f32[112,128]{1,0:T(8,128)S(1)}, u32[]{:S(2)}, u32[]{:S(2)}) collective-permute-start(f32[112,128]{1,0:T(8,128)S(1)} %get-tuple-element.84), channel_id=1, source_target_pairs={{0,4},{1,5},{2,6},{3,7},{4,0},{5,1},{6,2},{7,3},{8,12},{9,13},{10,... | collective-permute-start | bytes 172040 | tf_op jit(solution)/shard_map/ppermute | solution.py:606
  21.3 0.2 collective-permute-start.5
  21.5 0.0 collective-permute-done.6.refs_2_
  21.5 1.5 %collective-permute-start.7 = (f32[16,256]{1,0:T(8,128)S(1)}, f32[16,256]{1,0:T(8,128)S(1)}, u32[]{:S(2)}, u32[]{:S(2)}) collective-permute-start(f32[16,256]{1,0:T(8,128)S(1)} %pad_maximum_fusion.1), channel_id=1, source_target_pairs={{0,2},{1,3},{2,0},{3,1},{4,6},{5,7},{6,4},{7,5},{8,10},{9,11},{10,... | collective-permute-start | bytes 49160 | tf_op jit(solution)/shard_map/ppermute | solution.py:610
  23.0 1.5 %shard_map.139 = (f32[9,56,128]{2,1,0:T(8,128)S(1)}, f32[216,512]{1,0:T(8,128)S(1)}, f32[96,1152]{1,0:T(8,128)S(1)}) custom-call(f32[9,56,128]{2,1,0:T(8,128)S(1)} %get-tuple-element.88.refs_0_, f32[9,56,128]{2,1,0:T(8,128)S(1)} %get-tuple-element.89.refs_1_, f32[328,128]{1,0:T(8,128)S(1)} %get-tuple-element.66.refs_10_.refs_13_.refs_2_, ...), custom_call_target="tpu_custom_call" | custom-call | flops 30000000 | bytes 2000000 | tf_op jit(solution)/shard_map/pallas_call | solution.py:578
  24.5 0.8 %collective-permute-done.7.refs_3_ = f32[16,256]{1,0:T(8,128)S(1)} collective-permute-done((f32[16,256]{1,0:T(8,128)S(1)}, f32[16,256]{1,0:T(8,128)S(1)}, u32[]{:S(2)}, u32[]{:S(2)}) %collective-permute-start.7) | collective-permute-done | bytes 16416 | tf_op jit(solution)/shard_map/ppermute | solution.py:610
  25.3 0.0 collective-permute-done.4.refs_0_
  25.3 0.0 collective-permute-done.5.refs_1_
  25.3 1.7 %shard_map.140 = f32[9,56,128]{2,1,0:T(8,128)} custom-call(f32[112,128]{1,0:T(8,128)S(1)} %collective-permute-done.4.refs_0_, f32[112,128]{1,0:T(8,128)S(1)} %collective-permute-done.5.refs_1_, f32[16,256]{1,0:T(8,128)S(1)} %collective-permute-done.6.refs_2_, f32[16,256]{1,0:T(8,128)S(1)} %collective-permute-done.7.refs_3_, ...), custom_call_target="tpu_custom_call" | custom-call | flops 10000000 | bytes 2000000 | tf_op jit(solution)/shard_map/pallas_call | solution.py:578
  (4 shorter events, 0.0 us)
Async XLA Ops:
  5.9 3.3 %collective-permute-start.2 = (f32[16,256]{1,0:T(8,128)S(1)}, f32[16,256]{1,0:T(8,128)S(1)}, u32[]{:S(2)}, u32[]{:S(2)}) collective-permute-start(f32[16,256]{1,0:T(8,128)S(1)} %get-tuple-element.54), channel_id=1, source_target_pairs={{0,1},{1,0},{2,3},{3,2},{4,5},{5,4},{6,7},{7,6},{8,9},{9,8},{10,11... | collective-permute-start | bytes 49160 | tf_op jit(solution)/shard_map/ppermute | solution.py:604
  6.4 6.6 %collective-permute-start = (f32[112,128]{1,0:T(8,128)S(1)}, f32[112,128]{1,0:T(8,128)S(1)}, u32[]{:S(2)}, u32[]{:S(2)}) collective-permute-start(f32[112,128]{1,0:T(8,128)S(1)} %get-tuple-element.52), channel_id=1, source_target_pairs={{0,4},{1,5},{2,6},{3,7},{4,0},{5,1},{6,2},{7,3},{8,12},{9,13},{10,... | collective-permute-start | bytes 172040 | tf_op jit(solution)/shard_map/ppermute | solution.py:606
  9.0 4.0 %collective-permute-start.1 = (f32[112,128]{1,0:T(8,128)S(1)}, f32[112,128]{1,0:T(8,128)S(1)}, u32[]{:S(2)}, u32[]{:S(2)}) collective-permute-start(f32[112,128]{1,0:T(8,128)S(1)} %get-tuple-element.53), channel_id=1, source_target_pairs={{0,1},{1,0},{2,3},{3,2},{4,8},{5,9},{6,10},{7,11},{8,4},{9,5},{10,... | collective-permute-start | bytes 172040 | tf_op jit(solution)/shard_map/ppermute | solution.py:605
  9.2 3.8 %collective-permute-start.3 = (f32[16,256]{1,0:T(8,128)S(1)}, f32[16,256]{1,0:T(8,128)S(1)}, u32[]{:S(2)}, u32[]{:S(2)}) collective-permute-start(f32[16,256]{1,0:T(8,128)S(1)} %pad_maximum_fusion), channel_id=1, source_target_pairs={{0,2},{1,3},{2,0},{3,1},{4,6},{5,7},{6,4},{7,5},{8,10},{9,11},{10,... | collective-permute-start | bytes 49160 | tf_op jit(solution)/shard_map/ppermute | solution.py:610
  18.3 3.2 %collective-permute-start.6 = (f32[16,256]{1,0:T(8,128)S(1)}, f32[16,256]{1,0:T(8,128)S(1)}, u32[]{:S(2)}, u32[]{:S(2)}) collective-permute-start(f32[16,256]{1,0:T(8,128)S(1)} %get-tuple-element.86), channel_id=1, source_target_pairs={{0,1},{1,0},{2,3},{3,2},{4,5},{5,4},{6,7},{7,6},{8,9},{9,8},{10,11... | collective-permute-start | bytes 49160 | tf_op jit(solution)/shard_map/ppermute | solution.py:604
  18.5 6.8 %collective-permute-start.4 = (f32[112,128]{1,0:T(8,128)S(1)}, f32[112,128]{1,0:T(8,128)S(1)}, u32[]{:S(2)}, u32[]{:S(2)}) collective-permute-start(f32[112,128]{1,0:T(8,128)S(1)} %get-tuple-element.84), channel_id=1, source_target_pairs={{0,4},{1,5},{2,6},{3,7},{4,0},{5,1},{6,2},{7,3},{8,12},{9,13},{10,... | collective-permute-start | bytes 172040 | tf_op jit(solution)/shard_map/ppermute | solution.py:606
  21.3 4.0 %collective-permute-start.5 = (f32[112,128]{1,0:T(8,128)S(1)}, f32[112,128]{1,0:T(8,128)S(1)}, u32[]{:S(2)}, u32[]{:S(2)}) collective-permute-start(f32[112,128]{1,0:T(8,128)S(1)} %get-tuple-element.85), channel_id=1, source_target_pairs={{0,1},{1,0},{2,3},{3,2},{4,8},{5,9},{6,10},{7,11},{8,4},{9,5},{10,... | collective-permute-start | bytes 172040 | tf_op jit(solution)/shard_map/ppermute | solution.py:605
  21.5 3.8 %collective-permute-start.7 = (f32[16,256]{1,0:T(8,128)S(1)}, f32[16,256]{1,0:T(8,128)S(1)}, u32[]{:S(2)}, u32[]{:S(2)}) collective-permute-start(f32[16,256]{1,0:T(8,128)S(1)} %pad_maximum_fusion.1), channel_id=1, source_target_pairs={{0,2},{1,3},{2,0},{3,1},{4,6},{5,7},{6,4},{7,5},{8,10},{9,11},{10,... | collective-permute-start | bytes 49160 | tf_op jit(solution)/shard_map/ppermute | solution.py:610

commit v4 on v3

--- a/solution.py
+++ b/solution.py
@@ -21,7 +21,7 @@
 I32 = jnp.int32
 
 Sizes = collections.namedtuple(
-    "Sizes", ["variables", "basis", "sub_count", "cap_sub", "rows", "half_rows"]
+    "Sizes", ["variables", "basis", "sub_count", "cap_sub", "rows", "half_rows", "ghosts"]
 )
 
 
@@ -65,9 +65,13 @@
     return jnp.concatenate(out, axis=1) if len(out) > 1 else out[0]
 
 
-def mix_group(moved_ref, star_ref, sizes, g):
+def order_after(x):
+    return split(x)[1].astype(F32) * 0.0
+
+
+def mix_group(moved_ref, star_ref, sizes, g, zero=None):
     basis, variables = sizes.basis, sizes.variables
-    acc = [None] * GROUP
+    acc = [zero] * GROUP
     for q in range(variables):
         for d in range(3):
             block = moved_ref[d * basis : (d + 1) * basis, q * 128 : (q + 1) * 128]
@@ -99,8 +103,10 @@
 
 
 def advance(src_ref, dst_ref, star_ref, left, sizes, emit, between):
+    zero = None
     for g in groups(sizes):
-        acc = mix_group(src_ref, star_ref, sizes, g)
+        acc = mix_group(src_ref, star_ref, sizes, g, zero)
+        zero = order_after(acc[-1])
         for i in range(GROUP):
             emit(g * GROUP + i, acc[i])
         dst_ref[:, group_lanes(g)] = dot(left, stack_right(acc))[: dst_ref.shape[0]]
@@ -215,26 +221,25 @@
         pk_refs[i][...] = block(k)
 
 
-def unpack(ins, slot_ref, sizes):
-    ra_ref, rb_ref, r1_ref, rk_refs = ins
-    ra, rb = ra_ref[...], rb_ref[...]
-    low = low_lanes(ra.shape)
-    top = jnp.where(low, ra, pltpu.roll(rb, CAP_DOM, 1))
-    bottom = jnp.where(low, pltpu.roll(ra, CAP_DOM, 1), rb)
-    dom = jnp.concatenate([top, bottom], axis=0)
+def by_rows(received):
+    return jnp.concatenate([received, pltpu.roll(received, CAP_DOM, 1)], axis=0)
+
+
+def with_subs(dom, r1_ref, rk_refs, slot_ref, sizes):
     me = lax.axis_index("sub")
     cap = sizes.cap_sub
     slot_ref[...] = jnp.zeros_like(slot_ref)
 
     def put(k, value):
-        slot_ref[pl.ds(pl.multiple_of(jnp.bitwise_xor(me, k) * cap, 8), cap), :] = value
+        start = pl.multiple_of(CAP_DOM + jnp.bitwise_xor(me, k) * cap, 8)
+        slot_ref[pl.ds(start, cap), :] = value
 
     put(1, r1_ref[0:cap, :])
     for i, k in enumerate(range(2, sizes.sub_count, 2)):
         put(k, rk_refs[i][0:cap, :])
         put(k + 1, rk_refs[i][cap : 2 * cap, :])
     sub = jnp.transpose(slot_ref[...], (1, 0))[: dom.shape[0]]
-    return jnp.concatenate([dom, sub], axis=1)
+    return jnp.where(low_lanes(dom.shape), dom, sub)
 
 
 def turn_blocks(values, left, turns):
@@ -361,6 +366,31 @@
             comb_ref[rows, p * 128 : (p + 1) * 128] = acc[p]
 
 
+def near_part(proj_ref, minus_ref, gath_ref, plus_ref, comb_ref, sizes):
+    variables = sizes.variables
+    for f in range(4):
+        rows = slice(f * PAD, (f + 1) * PAD)
+        acc = [None] * variables
+        for q in range(variables):
+            own = proj_ref[rows, q * 128 : (q + 1) * 128]
+            other = gath_ref[q * PAD : (q + 1) * PAD, f * 128 : (f + 1) * 128]
+            for p in range(variables):
+                row = (q * variables + p) * 4 + f
+                term = own * minus_ref[row : row + 1, :]
+                acc[p] = term if acc[p] is None else acc[p] + term
+                acc[p] = acc[p] + other * plus_ref[row : row + 1, :]
+        for p in range(variables):
+            comb_ref[rows, p * 128 : (p + 1) * 128] = acc[p]
+
+
+def plus_by_slot(plus_ref, ghost_pick_ref, out_ref, sizes):
+    mats = sizes.variables**2
+    pieces = [pad_to(plus_ref[pl.ds(f, mats, stride=4), :], out_ref.shape[0], 128) for f in range(4)]
+    high, low = split(jnp.concatenate(pieces, axis=1))
+    pick = ghost_pick_ref[...]
+    out_ref[...] = dot_nt(high, pick) + dot_nt(low, pick)
+
+
 def kernel_local_first(sizes, *refs):
     (class_ref, minus_table, plus_table, code_ref, flux_ref, stiff_ref, lift_ref, orient_ref,
      first_ref, state_ref, star_ref, proj_ref, faces_ref,
@@ -385,9 +415,11 @@
                 (place + j * 128 == target[f : f + 1, :]).astype(F32).astype(BF16)
             )
     slot = code - 128
-    swapped = jnp.where(slot < CAP_DOM, slot + CAP_DOM, jnp.where(slot < 2 * CAP_DOM, slot - CAP_DOM, slot))
-    slot = jnp.where(is_even(), swapped, slot)
-    slot = jnp.where(code < 128, -1, slot)
+    swapped = jnp.where(slot < CAP_DOM, slot + CAP_DOM, slot - CAP_DOM)
+    dom_slot = jnp.where(is_even(), swapped, slot)
+    dom_slot = jnp.where(dom_slot < CAP_DOM, dom_slot, dom_slot + CAP_DOM)
+    slot = jnp.where(slot < 2 * CAP_DOM, dom_slot, slot + CAP_DOM)
+    slot = jnp.where(jnp.logical_or(code < 128, code >= 128 + sizes.ghosts), -1, slot)
     for f in range(4):
         for j in range(2):
             ghost_pick_ref[j * 128 : (j + 1) * 128, f * 128 : (f + 1) * 128] = (
@@ -396,8 +428,8 @@
     rows = jnp.broadcast_to(turn_row.astype(F32), (16, 512)).astype(BF16)
     ghost_turn_ref[...] = dot_nt(rows, ghost_pick_ref[...])[0:1].astype(I32)
     interior_part(faces_ref, pick_ref, oleft_ref[...], turn_row, gath_ref, sizes)
+    lookup(plus_table, stage_ref, class_ref[...], plus_ref)
     own_part(proj_ref, minus_ref, comb_ref, sizes)
-    lookup(plus_table, stage_ref, class_ref[...], plus_ref)
     lstage_ref[...] = jnp.zeros_like(lstage_ref)
     for f in range(4):
         lstage_ref[f * PAD : f * PAD + lift_ref.shape[0], :basis] = lift_ref[:, f, :]
@@ -412,17 +444,74 @@
 
 
 def kernel_local_second(sizes, *refs):
-    (second_ref, middle_ref, star_ref, kleft_ref, proj_ref, faces_ref, minus_ref, oleft_ref, pick_ref, turn_ref,
-     partial_ref, gath_ref, comb_ref, moved_ref) = refs
+    (second_ref, middle_ref, star_ref, kleft_ref, proj_ref, faces_ref, minus_ref, plus_ref, oleft_ref, pick_ref,
+     turn_ref, ghost_pick_ref, partial_ref, comb_ref, slot_plus_ref, moved_ref, gath_ref) = refs
     volume_part(second_ref, middle_ref, star_ref, kleft_ref[...], moved_ref, partial_ref, sizes)
     interior_part(faces_ref, pick_ref, oleft_ref[...], turn_ref[...], gath_ref, sizes)
-    own_part(proj_ref, minus_ref, comb_ref, sizes)
-
-
-def neighbour_part(ins, oleft_ref, ghost_turn_ref, ghost_pick_ref, gath_ref, comb_ref, plus_ref, lleft_ref, llow_ref,
+    near_part(proj_ref, minus_ref, gath_ref, plus_ref, comb_ref, sizes)
+    plus_by_slot(plus_ref, ghost_pick_ref, slot_plus_ref, sizes)
+
+
+def ghost_side(received, tile, oleft_ref, ghost_turn_ref, ghost_pick_ref, slot_plus_ref, ghost_ref, comb_ref, sizes):
+    variables, rows = sizes.variables, sizes.rows
+    lanes = slice(tile * 128, (tile + 1) * 128)
+    blocks = [received[q * PAD : (q + 1) * PAD] for q in range(variables)]
+    turned = turn_blocks(blocks, oleft_ref[...], ghost_turn_ref[:, lanes])
+    acc = [None] * variables
+    for q in range(variables):
+        for p in range(variables):
+            row = q * variables + p
+            term = turned[q] * slot_plus_ref[row : row + 1, lanes]
+            acc[p] = term if acc[p] is None else acc[p] + term
+    high, low = split(pad_to(jnp.concatenate(acc, axis=0), rows, 128))
+    ghost_ref[0:rows, :] = high
+    ghost_ref[rows : 2 * rows, :] = low
+    both = dot(ghost_ref[...], ghost_pick_ref[lanes, :])
+    out = []
+    for p in range(variables):
+        pieces = []
+        for f in range(4):
+            cols = slice(f * 128, (f + 1) * 128)
+            spread = both[p * PAD : (p + 1) * PAD, cols] + both[rows + p * PAD : rows + (p + 1) * PAD, cols]
+            pieces.append(comb_ref[f * PAD : (f + 1) * PAD, p * 128 : (p + 1) * 128] + spread)
+        out.append(jnp.concatenate(pieces, axis=0))
+    return out
+
+
+def kernel_even(sizes, *refs):
+    (ra_ref, oleft_ref, ghost_turn_ref, ghost_pick_ref, slot_plus_ref, comb_ref, out_ref, ghost_ref) = refs
+    values = ghost_side(by_rows(ra_ref[...]), 0, oleft_ref, ghost_turn_ref, ghost_pick_ref, slot_plus_ref,
+                        ghost_ref, comb_ref, sizes)
+    for p in range(sizes.variables):
+        out_ref[:, p * 128 : (p + 1) * 128] = values[p]
+
+
+def neighbour_part(ins, oleft_ref, ghost_turn_ref, ghost_pick_ref, slot_plus_ref, comb_ref, lleft_ref, llow_ref,
+                   partial_ref, slot_ref, ghost_ref, sizes):
+    basis = sizes.basis
+    rb_ref, r1_ref, rk_refs = ins
+    received = with_subs(by_rows(rb_ref[...]), r1_ref, rk_refs, slot_ref, sizes)
+    faces = ghost_side(received, 1, oleft_ref, ghost_turn_ref, ghost_pick_ref, slot_plus_ref, ghost_ref, comb_ref, sizes)
+    highs, stacks = [], []
+    for value in faces:
+        high, low = split(value)
+        highs.append(high)
+        stacks.append(jnp.concatenate([high, low], axis=0))
+    lifted = dot(lleft_ref[:, : 8 * PAD], jnp.concatenate(stacks, axis=1)) + dot(
+        llow_ref[:, : 4 * PAD], jnp.concatenate(highs, axis=1)
+    )
+    for g in groups(sizes):
+        yield g, [
+            partial_ref[p] + lifted[:basis, p * 128 : (p + 1) * 128] for p in range(g * GROUP, (g + 1) * GROUP)
+        ]
+
+
+def neighbour_all(ins, oleft_ref, ghost_turn_ref, ghost_pick_ref, gath_ref, comb_ref, plus_ref, lleft_ref, llow_ref,
                    partial_ref, slot_ref, ghost_ref, gsum_ref, sizes):
     variables, basis, rows = sizes.variables, sizes.basis, sizes.rows
-    received = unpack(ins, slot_ref, sizes)
+    ra_ref, rb_ref, r1_ref, rk_refs = ins
+    received = [by_rows(ra_ref[...]), with_subs(by_rows(rb_ref[...]), r1_ref, rk_refs, slot_ref, sizes)]
+    received = jnp.concatenate(received, axis=1)
     blocks = [received[q * PAD : (q + 1) * PAD] for q in range(variables)]
     turned = turn_blocks(blocks, oleft_ref[...], ghost_turn_ref[...])
     high, low = split(pad_to(jnp.concatenate(turned, axis=0), rows, turned[0].shape[1]))
@@ -470,7 +559,7 @@
     pk_refs, rest = rest[:xs], rest[xs:]
     moved_ref, other_ref, slot_ref, pslot_ref, ghost_ref, gsum_ref = rest
     left = dleft_ref[...]
-    for g, values in neighbour_part((ra_ref, rb_ref, r1_ref, rk_refs), oleft_ref, ghost_turn_ref, ghost_pick_ref,
+    for g, values in neighbour_all((ra_ref, rb_ref, r1_ref, rk_refs), oleft_ref, ghost_turn_ref, ghost_pick_ref,
                                     gath_ref, comb_ref, plus_ref, lleft_ref, llow_ref, partial_ref, slot_ref,
                                     ghost_ref, gsum_ref, sizes):
         moved_ref[:, group_lanes(g)] = dot(left, stack_right(values))[: moved_ref.shape[0]]
@@ -492,14 +581,14 @@
 
 def kernel_last(sizes, *refs):
     xs = sizes.sub_count // 2 - 1
-    ra_ref, rb_ref, r1_ref, *refs = refs
+    rb_ref, r1_ref, *refs = refs
     rk_refs, refs = refs[:xs], refs[xs:]
-    (oleft_ref, ghost_turn_ref, ghost_pick_ref, gath_ref, comb_ref, plus_ref, lleft_ref, llow_ref, partial_ref,
-     out_hbm, slot_ref, ghost_ref, gsum_ref, out_ref, sems) = refs
+    (oleft_ref, ghost_turn_ref, ghost_pick_ref, slot_plus_ref, comb_ref, lleft_ref, llow_ref, partial_ref,
+     out_hbm, slot_ref, ghost_ref, out_ref, sems) = refs
     copies = []
-    for g, values in neighbour_part((ra_ref, rb_ref, r1_ref, rk_refs), oleft_ref, ghost_turn_ref, ghost_pick_ref,
-                                    gath_ref, comb_ref, plus_ref, lleft_ref, llow_ref, partial_ref, slot_ref,
-                                    ghost_ref, gsum_ref, sizes):
+    for g, values in neighbour_part((rb_ref, r1_ref, rk_refs), oleft_ref, ghost_turn_ref, ghost_pick_ref,
+                                    slot_plus_ref, comb_ref, lleft_ref, llow_ref, partial_ref, slot_ref,
+                                    ghost_ref, sizes):
         for i in range(GROUP):
             out_ref[g * GROUP + i] = values[i]
         part = pl.ds(g * GROUP, GROUP)
@@ -533,7 +622,7 @@
     lanes = variables * elements
     half_rows = -(-variables * PAD // 32) * 16
     rows = 2 * half_rows
-    sizes = Sizes(variables, basis, sub_count, cap_sub, rows, half_rows)
+    sizes = Sizes(variables, basis, sub_count, cap_sub, rows, half_rows, ghosts)
     sub_lanes = -(-rows // 128) * 128
     mat_rows = variables * variables * 4 + 4
     xs = sub_count // 2 - 1
@@ -569,7 +658,9 @@
     stage_s = pltpu.VMEM((mat_rows, 128), F32)
     slot_s = pltpu.VMEM((128, sub_lanes), F32)
     pslot_s = pltpu.VMEM((ghosts - 2 * CAP_DOM, sub_lanes), F32)
-    ghost_s = pltpu.VMEM((2 * rows, 256), BF16)
+    ghost_s = pltpu.VMEM((2 * rows, 128), BF16)
+    ghost_all_s = pltpu.VMEM((2 * rows, 256), BF16)
+    slot_mat_t = sds(-(-variables * variables // 16) * 16, 256)
 
     def call(fn, outs, scratches, operands, flops, space=pltpu.VMEM, out_space=pltpu.VMEM):
         vmem = pl.BlockSpec(memory_space=out_space)
@@ -629,7 +720,7 @@
     classes = outs[0]
     state, first, late, proj, faces, star, dleft, rleft, pick_send, pick_sub, *payload = outs[9:]
     received = trade(payload)
-    (partial, gath, comb, minus, plus, kleft, oleft, lleft, llow, pick, ghost_pick, turn, ghost_turn) = call(
+    partial, gath, comb, minus, plus, kleft, oleft, lleft, llow, pick, ghost_pick, turn, ghost_turn = call(
         kernel_local_first,
         [whole, gath_t, face_t, mat_t, mat_t, left_t, sds(80, 3 * OSEC, dtype=BF16)]
         + [sds(64, 256, dtype=BF16), sds(64, 128, dtype=BF16)]
@@ -643,25 +734,27 @@
     middle, second, proj, faces, *payload = call(
         kernel_second,
         [whole, whole, face_t, faces_t] + pay_t,
-        [moved_s, moved_s, slot_s, pslot_s, ghost_s, scratch(gath_t)],
+        [moved_s, moved_s, slot_s, pslot_s, ghost_all_s, scratch(gath_t)],
         received
         + common
         + [gath, comb, plus, lleft, llow, partial, star, late, clusters, dleft, rleft, pick_send, pick_sub],
         70_000_000,
     )
     received = trade(payload)
-    partial, gath, comb = call(
+    partial, comb, slot_plus = call(
         kernel_local_second,
-        [whole, gath_t, face_t],
-        [moved_s],
-        [second, middle, star, kleft, proj, faces, minus, oleft, pick, turn],
+        [whole, face_t, slot_mat_t],
+        [moved_s, scratch(gath_t)],
+        [second, middle, star, kleft, proj, faces, minus, plus, oleft, pick, turn, ghost_pick],
         30_000_000,
     )
+    common = [*common, slot_plus]
+    comb = call(kernel_even, face_t, [ghost_s], [received[0], *common, comb], 3_000_000)
     result = call(
         kernel_last,
         whole,
-        [slot_s, ghost_s, scratch(gath_t), scratch(whole), pltpu.SemaphoreType.DMA((variables // GROUP,))],
-        received + common + [gath, comb, plus, lleft, llow, partial],
+        [slot_s, ghost_s, scratch(whole), pltpu.SemaphoreType.DMA((variables // GROUP,))],
+        received[1:] + common + [comb, lleft, llow, partial],
         10_000_000,
         out_space=pltpu.HBM,
     )

time: 27.2 us -> 26.9 us (0.989)
  waiting for transfers between devices: 0.83 us -> 0.02 us
  Pallas kernels: 16.7 us -> 17.1 us
    ppermute x2, waiting for transfers between devices: 0.81 us -> 0.01 us  [trade(): lax.ppermute(jnp.concatenate([part, passed], axis=0), combined, sub_pairs...]
    pallas_call x5 -> x6, Pallas kernels: 16.7 us -> 17.1 us  [call(): pl.pallas_call(functools.partial(fn, sizes), out_shape=outs, in_specs=[pl...]
  transfers between devices with their start and end apart: 8 -> 8, of which waited for: 1 -> 0; matrix products, arithmetic and copies ran while one was open for 0% -> 0% of each run, Pallas kernels for 14% -> 17%
where the time goes in v4:
time: 26.9 us; the launch traced here: 26.8 us
  Pallas kernels  17.1 us (64%)
  starting transfers between devices  9.51 us (35%)
    pallas_call x6, Pallas kernels, call(): pl.pallas_call(functools.partial(fn, sizes), out_shape=outs, in_specs=[pl...  17.1 us
    ppermute x2, starting transfers between devices, trade(): ra = lax.ppermute(pa, combined, even_pairs)  5.5 us
    ppermute x2, starting transfers between devices, trade(): lax.ppermute(jnp.concatenate([part, passed], axis=0), combined, sub_pairs...  3.02 us
    ppermute x2, starting transfers between devices, trade(): r1 = lax.ppermute(p1, combined, sub_pairs(1))  0.65 us
  transfers between devices with their start and end apart: 8, of which 0 were waited for; matrix products, arithmetic and copies ran while one was open for 0% of the time, Pallas kernels for 17%

profile of v4, /device:TPU:0, one launch (start us, length us, event | category | flops | bytes accessed | tf_op | source)
XLA Modules:
  0.0 26.8 jit_solution(8644440496667743369)
XLA Ops:
  0.0 5.9 %shard_map.136 = (s32[1,128]{1,0:T(1,128)S(1)}, s32[1,128]{1,0:T(1,128)S(1)}, f32[9,9,4,64]{3,2,1,0:T(4,128)S(1)}, f32[9,9,4,64]{3,2,1,0:T(4,128)S(1)}, s32[4,12...) custom-call(f32[9,56,128]{2,1,0:T(8,128)} %bitcast.10, ...), custom_call_target="tpu_custom_call" | custom-call | flops 60000000 | bytes 2000000 | tf_op jit(solution)/shard_map/pallas_call | solution.py:669
  5.9 0.5 %collective-permute-start.2 = (f32[16,256]{1,0:T(8,128)S(1)}, f32[16,256]{1,0:T(8,128)S(1)}, u32[]{:S(2)}, u32[]{:S(2)}) collective-permute-start(f32[16,256]{1,0:T(8,128)S(1)} %get-tuple-element.54), channel_id=1, source_target_pairs={{0,1},{1,0},{2,3},{3,2},{4,5},{5,4},{6,7},{7,6},{8,9},{9,8},{10,11... | collective-permute-start | bytes 49160 | tf_op jit(solution)/shard_map/ppermute | solution.py:695
  6.4 2.6 %collective-permute-start = (f32[112,128]{1,0:T(8,128)S(1)}, f32[112,128]{1,0:T(8,128)S(1)}, u32[]{:S(2)}, u32[]{:S(2)}) collective-permute-start(f32[112,128]{1,0:T(8,128)S(1)} %get-tuple-element.52), channel_id=1, source_target_pairs={{0,4},{1,5},{2,6},{3,7},{4,0},{5,1},{6,2},{7,3},{8,12},{9,13},{10,... | collective-permute-start | bytes 172040 | tf_op jit(solution)/shard_map/ppermute | solution.py:697
  9.0 0.2 collective-permute-start.1
  9.2 0.0 collective-permute-done.2.refs_2_
  9.2 1.6 %collective-permute-start.3 = (f32[16,256]{1,0:T(8,128)S(1)}, f32[16,256]{1,0:T(8,128)S(1)}, u32[]{:S(2)}, u32[]{:S(2)}) collective-permute-start(f32[16,256]{1,0:T(8,128)S(1)} %pad_maximum_fusion), channel_id=1, source_target_pairs={{0,2},{1,3},{2,0},{3,1},{4,6},{5,7},{6,4},{7,5},{8,10},{9,11},{10,... | collective-permute-start | bytes 49160 | tf_op jit(solution)/shard_map/ppermute | solution.py:701
  10.7 2.3 %shard_map.137 = (f32[9,56,128]{2,1,0:T(8,128)S(1)}, f32[216,512]{1,0:T(8,128)S(1)}, f32[96,1152]{1,0:T(8,128)S(1)}, f32[328,128]{1,0:T(8,128)S(1)}, f32[328,128...) custom-call(s32[1,128]{1,0:T(1,128)S(1)} %get-tuple-element.56.refs_, ...), custom_call_target="tpu_custom_call" | custom-call | flops 30000000 | bytes 2000000 | tf_op jit(solution)/shard_map/pallas_call | solution.py:669
  13.0 0.0 collective-permute-done.3.refs_3_
  13.0 0.0 collective-permute-done.refs_0_
  13.0 0.0 collective-permute-done.1.refs_1_
  13.0 5.2 %shard_map.138 = (f32[9,56,128]{2,1,0:T(8,128)S(1)}, f32[9,56,128]{2,1,0:T(8,128)S(1)}, f32[96,1152]{1,0:T(8,128)S(1)}, bf16[448,512]{1,0:T(8,128)(2,1)S(1)}, f3...) custom-call(f32[112,128]{1,0:T(8,128)S(1)} %collective-permute-done.refs_0_, ...), custom_call_target="tpu_custom_call" | custom-call | flops 70000000 | bytes 2000000 | tf_op jit(solution)/shard_map/pallas_call | solution.py:669
  18.2 0.1 collective-permute-start.5
  18.3 2.9 %collective-permute-start.7 = (f32[112,128]{1,0:T(8,128)S(1)}, f32[112,128]{1,0:T(8,128)S(1)}, u32[]{:S(2)}, u32[]{:S(2)}) collective-permute-start(f32[112,128]{1,0:T(8,128)S(1)} %get-tuple-element.96), channel_id=1, source_target_pairs={{0,4},{1,5},{2,6},{3,7},{4,0},{5,1},{6,2},{7,3},{8,12},{9,13},{10,... | collective-permute-start | bytes 172040 | tf_op jit(solution)/shard_map/ppermute | solution.py:697
  21.2 0.2 collective-permute-start.4
  21.4 0.0 collective-permute-done.5.refs_1_
  21.4 1.5 %collective-permute-start.6 = (f32[16,256]{1,0:T(8,128)S(1)}, f32[16,256]{1,0:T(8,128)S(1)}, u32[]{:S(2)}, u32[]{:S(2)}) collective-permute-start(f32[16,256]{1,0:T(8,128)S(1)} %pad_maximum_fusion.1), channel_id=1, source_target_pairs={{0,2},{1,3},{2,0},{3,1},{4,6},{5,7},{6,4},{7,5},{8,10},{9,11},{10,... | collective-permute-start | bytes 49160 | tf_op jit(solution)/shard_map/ppermute | solution.py:701
  22.9 1.8 %shard_map.139 = (f32[9,56,128]{2,1,0:T(8,128)S(1)}, f32[96,1152]{1,0:T(8,128)S(1)}, f32[96,256]{1,0:T(8,128)S(1)}) custom-call(f32[9,56,128]{2,1,0:T(8,128)S(1)} %get-tuple-element.87.refs_0_, f32[9,56,128]{2,1,0:T(8,128)S(1)} %get-tuple-element.88.refs_1_, f32[328,128]{1,0:T(8,128)S(1)} %get-tuple-element.66.refs_10_.refs_13_.refs_2_, ...), custom_call_target="tpu_custom_call" | custom-call | flops 30000000 | bytes 2000000 | tf_op jit(solution)/shard_map/pallas_call | solution.py:669
  24.7 0.0 collective-permute-done.7.refs_0_
  24.8 0.5 %shard_map.140.refs_7_ = f32[96,1152]{1,0:T(8,128)S(1)} custom-call(f32[112,128]{1,0:T(8,128)S(1)} %collective-permute-done.7.refs_0_, bf16[80,96]{1,0:T(8,128)(2,1)S(1)} %get-tuple-element.69.refs_4_.refs_8_.refs_1_.refs_3_, s32[1,256]{1,0:T(1,128)S(1)} %get-tuple-element.70.refs_5_.refs_2_.refs_4_, ...), custom_call_target="tpu_custom_call" | custom-call | flops 3000000 | bytes 2000000 | tf_op jit(solution)/shard_map/pallas_call | solution.py:669
  25.3 0.0 collective-permute-done.6.refs_2_
  25.3 0.0 collective-permute-done.4.refs_0_
  25.3 1.5 %shard_map.141 = f32[9,56,128]{2,1,0:T(8,128)} custom-call(f32[112,128]{1,0:T(8,128)S(1)} %collective-permute-done.4.refs_0_, f32[16,256]{1,0:T(8,128)S(1)} %collective-permute-done.5.refs_1_, f32[16,256]{1,0:T(8,128)S(1)} %collective-permute-done.6.refs_2_, bf16[80,96]{1,0:T(8,128)(2,1)S(1)} %get-tuple-element.69.refs_4_.refs_8_.refs_1_.refs_3_, ...), custom_call_target="tpu_custom_call" | custom-call | flops 10000000 | bytes 2000000 | tf_op jit(solution)/shard_map/pallas_call | solution.py:669
  (4 shorter events, 0.0 us)
Async XLA Ops:
  5.9 3.3 %collective-permute-start.2 = (f32[16,256]{1,0:T(8,128)S(1)}, f32[16,256]{1,0:T(8,128)S(1)}, u32[]{:S(2)}, u32[]{:S(2)}) collective-permute-start(f32[16,256]{1,0:T(8,128)S(1)} %get-tuple-element.54), channel_id=1, source_target_pairs={{0,1},{1,0},{2,3},{3,2},{4,5},{5,4},{6,7},{7,6},{8,9},{9,8},{10,11... | collective-permute-start | bytes 49160 | tf_op jit(solution)/shard_map/ppermute | solution.py:695
  6.4 6.6 %collective-permute-start = (f32[112,128]{1,0:T(8,128)S(1)}, f32[112,128]{1,0:T(8,128)S(1)}, u32[]{:S(2)}, u32[]{:S(2)}) collective-permute-start(f32[112,128]{1,0:T(8,128)S(1)} %get-tuple-element.52), channel_id=1, source_target_pairs={{0,4},{1,5},{2,6},{3,7},{4,0},{5,1},{6,2},{7,3},{8,12},{9,13},{10,... | collective-permute-start | bytes 172040 | tf_op jit(solution)/shard_map/ppermute | solution.py:697
  9.0 4.0 %collective-permute-start.1 = (f32[112,128]{1,0:T(8,128)S(1)}, f32[112,128]{1,0:T(8,128)S(1)}, u32[]{:S(2)}, u32[]{:S(2)}) collective-permute-start(f32[112,128]{1,0:T(8,128)S(1)} %get-tuple-element.53), channel_id=1, source_target_pairs={{0,1},{1,0},{2,3},{3,2},{4,8},{5,9},{6,10},{7,11},{8,4},{9,5},{10,... | collective-permute-start | bytes 172040 | tf_op jit(solution)/shard_map/ppermute | solution.py:696
  9.2 3.8 %collective-permute-start.3 = (f32[16,256]{1,0:T(8,128)S(1)}, f32[16,256]{1,0:T(8,128)S(1)}, u32[]{:S(2)}, u32[]{:S(2)}) collective-permute-start(f32[16,256]{1,0:T(8,128)S(1)} %pad_maximum_fusion), channel_id=1, source_target_pairs={{0,2},{1,3},{2,0},{3,1},{4,6},{5,7},{6,4},{7,5},{8,10},{9,11},{10,... | collective-permute-start | bytes 49160 | tf_op jit(solution)/shard_map/ppermute | solution.py:701
  18.2 3.2 %collective-permute-start.5 = (f32[16,256]{1,0:T(8,128)S(1)}, f32[16,256]{1,0:T(8,128)S(1)}, u32[]{:S(2)}, u32[]{:S(2)}) collective-permute-start(f32[16,256]{1,0:T(8,128)S(1)} %get-tuple-element.85), channel_id=1, source_target_pairs={{0,1},{1,0},{2,3},{3,2},{4,5},{5,4},{6,7},{7,6},{8,9},{9,8},{10,11... | collective-permute-start | bytes 49160 | tf_op jit(solution)/shard_map/ppermute | solution.py:695
  18.3 6.4 %collective-permute-start.7 = (f32[112,128]{1,0:T(8,128)S(1)}, f32[112,128]{1,0:T(8,128)S(1)}, u32[]{:S(2)}, u32[]{:S(2)}) collective-permute-start(f32[112,128]{1,0:T(8,128)S(1)} %get-tuple-element.96), channel_id=1, source_target_pairs={{0,4},{1,5},{2,6},{3,7},{4,0},{5,1},{6,2},{7,3},{8,12},{9,13},{10,... | collective-permute-start | bytes 172040 | tf_op jit(solution)/shard_map/ppermute | solution.py:697
  21.2 4.0 %collective-permute-start.4 = (f32[112,128]{1,0:T(8,128)S(1)}, f32[112,128]{1,0:T(8,128)S(1)}, u32[]{:S(2)}, u32[]{:S(2)}) collective-permute-start(f32[112,128]{1,0:T(8,128)S(1)} %get-tuple-element.84), channel_id=1, source_target_pairs={{0,1},{1,0},{2,3},{3,2},{4,8},{5,9},{6,10},{7,11},{8,4},{9,5},{10,... | collective-permute-start | bytes 172040 | tf_op jit(solution)/shard_map/ppermute | solution.py:696
  21.4 3.9 %collective-permute-start.6 = (f32[16,256]{1,0:T(8,128)S(1)}, f32[16,256]{1,0:T(8,128)S(1)}, u32[]{:S(2)}, u32[]{:S(2)}) collective-permute-start(f32[16,256]{1,0:T(8,128)S(1)} %pad_maximum_fusion.1), channel_id=1, source_target_pairs={{0,2},{1,3},{2,0},{3,1},{4,6},{5,7},{6,4},{7,5},{8,10},{9,11},{10,... | collective-permute-start | bytes 49160 | tf_op jit(solution)/shard_map/ppermute | solution.py:701

commit v5 on v4

--- a/solution.py
+++ b/solution.py
@@ -520,26 +520,22 @@
     both = dot(ghost_ref[...], ghost_pick_ref[...])
     used = variables * PAD
     gsum_ref[...] = gath_ref[...] + (both[0:used] + both[rows : rows + used])
+    faces = [[] for _ in range(variables)]
+    for f in range(4):
+        frows = slice(f * PAD, (f + 1) * PAD)
+        acc = [comb_ref[frows, p * 128 : (p + 1) * 128] for p in range(variables)]
+        for q in range(variables):
+            block = gsum_ref[q * PAD : (q + 1) * PAD, f * 128 : (f + 1) * 128]
+            for p in range(variables):
+                row = (q * variables + p) * 4 + f
+                acc[p] = acc[p] + block * plus_ref[row : row + 1, :]
+        for p in range(variables):
+            faces[p].append(acc[p])
     highs, stacks = [], []
-    for g in groups(sizes):
-        faces = [[], [], []]
-        for f in range(4):
-            frows = slice(f * PAD, (f + 1) * PAD)
-            acc = []
-            for i in range(GROUP):
-                p = g * GROUP + i
-                acc.append(comb_ref[frows, p * 128 : (p + 1) * 128])
-            for q in range(variables):
-                block = gsum_ref[q * PAD : (q + 1) * PAD, f * 128 : (f + 1) * 128]
-                for i in range(GROUP):
-                    row = (q * variables + g * GROUP + i) * 4 + f
-                    acc[i] = acc[i] + block * plus_ref[row : row + 1, :]
-            for i in range(GROUP):
-                faces[i].append(acc[i])
-        for i in range(GROUP):
-            high, low = split(jnp.concatenate(faces[i], axis=0))
-            highs.append(high)
-            stacks.append(jnp.concatenate([high, low], axis=0))
+    for pieces in faces:
+        high, low = split(jnp.concatenate(pieces, axis=0))
+        highs.append(high)
+        stacks.append(jnp.concatenate([high, low], axis=0))
     lifted = dot(lleft_ref[:, : 8 * PAD], jnp.concatenate(stacks, axis=1)) + dot(
         llow_ref[:, : 4 * PAD], jnp.concatenate(highs, axis=1)
     )
@@ -693,12 +689,13 @@
     def trade(payload):
         pa, pb, p1, *pk = payload
         r1 = lax.ppermute(p1, combined, sub_pairs(1))
-        rb = lax.ppermute(pb, combined, odd_pairs)
         ra = lax.ppermute(pa, combined, even_pairs)
         rk = []
+        pb, r1 = lax.optimization_barrier((pb, r1))
         for i, part in enumerate(pk):
             passed = r1[(i + 1) * cap_sub : (i + 2) * cap_sub]
             rk.append(lax.ppermute(jnp.concatenate([part, passed], axis=0), combined, sub_pairs(2 * i + 2)))
+        rb = lax.ppermute(pb, combined, odd_pairs)
         return [ra, rb, r1, *rk]
 
     later = [clusters, minus_table, plus_table, face_neighbour, flux_index, stiffness, lift, orientation]

time: 26.9 us -> 26.8 us (level)
  no operation moved by 1% of the time
where the time goes in v5:
time: 26.8 us; the launch traced here: 26.6 us
  Pallas kernels  17.2 us (64%)
  starting transfers between devices  9.36 us (35%)
    pallas_call x6, Pallas kernels, call(): pl.pallas_call(functools.partial(fn, sizes), out_shape=outs, in_specs=[pl...  17.2 us
    ppermute x2, starting transfers between devices, trade(): ra = lax.ppermute(pa, combined, even_pairs)  5.49 us
    ppermute x2, starting transfers between devices, trade(): lax.ppermute(jnp.concatenate([part, passed], axis=0), combined, sub_pairs...  2.9 us
    ppermute x2, starting transfers between devices, trade(): r1 = lax.ppermute(p1, combined, sub_pairs(1))  0.64 us
  transfers between devices with their start and end apart: 8, of which 0 were waited for; matrix products, arithmetic and copies ran while one was open for 0% of the time, Pallas kernels for 17%

profile of v5, /device:TPU:0, one launch (start us, length us, event | category | flops | bytes accessed | tf_op | source)
XLA Modules:
  0.0 26.6 jit_solution(8819428008200954818)
XLA Ops:
  0.0 5.9 %shard_map.136 = (s32[1,128]{1,0:T(1,128)S(1)}, s32[1,128]{1,0:T(1,128)S(1)}, f32[9,9,4,64]{3,2,1,0:T(4,128)S(1)}, f32[9,9,4,64]{3,2,1,0:T(4,128)S(1)}, s32[4,12...) custom-call(f32[9,56,128]{2,1,0:T(8,128)} %bitcast.10, ...), custom_call_target="tpu_custom_call" | custom-call | flops 60000000 | bytes 2000000 | tf_op jit(solution)/shard_map/pallas_call | solution.py:665
  5.9 0.5 %collective-permute-start.1 = (f32[16,256]{1,0:T(8,128)S(1)}, f32[16,256]{1,0:T(8,128)S(1)}, u32[]{:S(2)}, u32[]{:S(2)}) collective-permute-start(f32[16,256]{1,0:T(8,128)S(1)} %get-tuple-element.58), channel_id=1, source_target_pairs={{0,1},{1,0},{2,3},{3,2},{4,5},{5,4},{6,7},{7,6},{8,9},{9,8},{10,11... | collective-permute-start | bytes 49160 | tf_op jit(solution)/shard_map/ppermute | solution.py:691
  6.4 2.6 %collective-permute-start = (f32[112,128]{1,0:T(8,128)S(1)}, f32[112,128]{1,0:T(8,128)S(1)}, u32[]{:S(2)}, u32[]{:S(2)}) collective-permute-start(f32[112,128]{1,0:T(8,128)S(1)} %get-tuple-element.56), channel_id=1, source_target_pairs={{0,4},{1,5},{2,6},{3,7},{4,0},{5,1},{6,2},{7,3},{8,12},{9,13},{10,... | collective-permute-start | bytes 172040 | tf_op jit(solution)/shard_map/ppermute | solution.py:692
  9.0 0.0 collective-permute-done.1.refs_2_
  9.0 0.2 collective-permute-start.2
  9.2 1.5 %collective-permute-start.3 = (f32[16,256]{1,0:T(8,128)S(1)}, f32[16,256]{1,0:T(8,128)S(1)}, u32[]{:S(2)}, u32[]{:S(2)}) collective-permute-start(f32[16,256]{1,0:T(8,128)S(1)} %pad_maximum_fusion), channel_id=1, source_target_pairs={{0,2},{1,3},{2,0},{3,1},{4,6},{5,7},{6,4},{7,5},{8,10},{9,11},{10,... | collective-permute-start | bytes 49160 | tf_op jit(solution)/shard_map/ppermute | solution.py:697
  10.7 2.3 %shard_map.137 = (f32[9,56,128]{2,1,0:T(8,128)S(1)}, f32[216,512]{1,0:T(8,128)S(1)}, f32[96,1152]{1,0:T(8,128)S(1)}, f32[328,128]{1,0:T(8,128)S(1)}, f32[328,128...) custom-call(s32[1,128]{1,0:T(1,128)S(1)} %get-tuple-element.62.refs_, ...), custom_call_target="tpu_custom_call" | custom-call | flops 30000000 | bytes 2000000 | tf_op jit(solution)/shard_map/pallas_call | solution.py:665
  13.0 0.0 collective-permute-done.3.refs_3_
  13.0 0.0 collective-permute-done.refs_0_
  13.0 0.0 collective-permute-done.2.refs_1_
  13.0 5.2 %shard_map.138 = (f32[9,56,128]{2,1,0:T(8,128)S(1)}, f32[9,56,128]{2,1,0:T(8,128)S(1)}, f32[96,1152]{1,0:T(8,128)S(1)}, bf16[448,512]{1,0:T(8,128)(2,1)S(1)}, f3...) custom-call(f32[112,128]{1,0:T(8,128)S(1)} %collective-permute-done.refs_0_, ...), custom_call_target="tpu_custom_call" | custom-call | flops 70000000 | bytes 2000000 | tf_op jit(solution)/shard_map/pallas_call | solution.py:665
  18.2 0.1 collective-permute-start.4
  18.3 2.9 %collective-permute-start.7 = (f32[112,128]{1,0:T(8,128)S(1)}, f32[112,128]{1,0:T(8,128)S(1)}, u32[]{:S(2)}, u32[]{:S(2)}) collective-permute-start(f32[112,128]{1,0:T(8,128)S(1)} %get-tuple-element.104), channel_id=1, source_target_pairs={{0,4},{1,5},{2,6},{3,7},{4,0},{5,1},{6,2},{7,3},{8,12},{9,13},{10,... | collective-permute-start | bytes 172040 | tf_op jit(solution)/shard_map/ppermute | solution.py:692
  21.2 0.0 collective-permute-done.4.refs_1_
  21.2 0.2 collective-permute-start.5
  21.4 1.4 %collective-permute-start.6 = (f32[16,256]{1,0:T(8,128)S(1)}, f32[16,256]{1,0:T(8,128)S(1)}, u32[]{:S(2)}, u32[]{:S(2)}) collective-permute-start(f32[16,256]{1,0:T(8,128)S(1)} %pad_maximum_fusion.1), channel_id=1, source_target_pairs={{0,2},{1,3},{2,0},{3,1},{4,6},{5,7},{6,4},{7,5},{8,10},{9,11},{10,... | collective-permute-start | bytes 49160 | tf_op jit(solution)/shard_map/ppermute | solution.py:697
  22.8 1.8 %shard_map.139 = (f32[9,56,128]{2,1,0:T(8,128)S(1)}, f32[96,1152]{1,0:T(8,128)S(1)}, f32[96,256]{1,0:T(8,128)S(1)}) custom-call(f32[9,56,128]{2,1,0:T(8,128)S(1)} %get-tuple-element.95.refs_0_, f32[9,56,128]{2,1,0:T(8,128)S(1)} %get-tuple-element.96.refs_1_, f32[328,128]{1,0:T(8,128)S(1)} %get-tuple-element.72.refs_10_.refs_13_.refs_2_, ...), custom_call_target="tpu_custom_call" | custom-call | flops 30000000 | bytes 2000000 | tf_op jit(solution)/shard_map/pallas_call | solution.py:665
  24.6 0.0 collective-permute-done.7.refs_0_
  24.6 0.5 %shard_map.140.refs_7_ = f32[96,1152]{1,0:T(8,128)S(1)} custom-call(f32[112,128]{1,0:T(8,128)S(1)} %collective-permute-done.7.refs_0_, bf16[80,96]{1,0:T(8,128)(2,1)S(1)} %get-tuple-element.75.refs_4_.refs_8_.refs_1_.refs_3_, s32[1,256]{1,0:T(1,128)S(1)} %get-tuple-element.76.refs_5_.refs_2_.refs_4_, ...), custom_call_target="tpu_custom_call" | custom-call | flops 3000000 | bytes 2000000 | tf_op jit(solution)/shard_map/pallas_call | solution.py:665
  25.1 0.0 collective-permute-done.6.refs_2_
  25.1 0.0 collective-permute-done.5.refs_0_
  25.2 1.5 %shard_map.141 = f32[9,56,128]{2,1,0:T(8,128)} custom-call(f32[112,128]{1,0:T(8,128)S(1)} %collective-permute-done.5.refs_0_, f32[16,256]{1,0:T(8,128)S(1)} %collective-permute-done.4.refs_1_, f32[16,256]{1,0:T(8,128)S(1)} %collective-permute-done.6.refs_2_, bf16[80,96]{1,0:T(8,128)(2,1)S(1)} %get-tuple-element.75.refs_4_.refs_8_.refs_1_.refs_3_, ...), custom_call_target="tpu_custom_call" | custom-call | flops 10000000 | bytes 2000000 | tf_op jit(solution)/shard_map/pallas_call | solution.py:665
  (4 shorter events, 0.0 us)
Async XLA Ops:
  5.9 3.1 %collective-permute-start.1 = (f32[16,256]{1,0:T(8,128)S(1)}, f32[16,256]{1,0:T(8,128)S(1)}, u32[]{:S(2)}, u32[]{:S(2)}) collective-permute-start(f32[16,256]{1,0:T(8,128)S(1)} %get-tuple-element.58), channel_id=1, source_target_pairs={{0,1},{1,0},{2,3},{3,2},{4,5},{5,4},{6,7},{7,6},{8,9},{9,8},{10,11... | collective-permute-start | bytes 49160 | tf_op jit(solution)/shard_map/ppermute | solution.py:691
  6.4 6.6 %collective-permute-start = (f32[112,128]{1,0:T(8,128)S(1)}, f32[112,128]{1,0:T(8,128)S(1)}, u32[]{:S(2)}, u32[]{:S(2)}) collective-permute-start(f32[112,128]{1,0:T(8,128)S(1)} %get-tuple-element.56), channel_id=1, source_target_pairs={{0,4},{1,5},{2,6},{3,7},{4,0},{5,1},{6,2},{7,3},{8,12},{9,13},{10,... | collective-permute-start | bytes 172040 | tf_op jit(solution)/shard_map/ppermute | solution.py:692
  9.0 4.0 %collective-permute-start.2 = (f32[112,128]{1,0:T(8,128)S(1)}, f32[112,128]{1,0:T(8,128)S(1)}, u32[]{:S(2)}, u32[]{:S(2)}) collective-permute-start(f32[112,128]{1,0:T(8,128)S(1)} %get-tuple-element.59), channel_id=1, source_target_pairs={{0,1},{1,0},{2,3},{3,2},{4,8},{5,9},{6,10},{7,11},{8,4},{9,5},{10,... | collective-permute-start | bytes 172040 | tf_op jit(solution)/shard_map/ppermute | solution.py:698
  9.2 3.8 %collective-permute-start.3 = (f32[16,256]{1,0:T(8,128)S(1)}, f32[16,256]{1,0:T(8,128)S(1)}, u32[]{:S(2)}, u32[]{:S(2)}) collective-permute-start(f32[16,256]{1,0:T(8,128)S(1)} %pad_maximum_fusion), channel_id=1, source_target_pairs={{0,2},{1,3},{2,0},{3,1},{4,6},{5,7},{6,4},{7,5},{8,10},{9,11},{10,... | collective-permute-start | bytes 49160 | tf_op jit(solution)/shard_map/ppermute | solution.py:697
  18.2 3.0 %collective-permute-start.4 = (f32[16,256]{1,0:T(8,128)S(1)}, f32[16,256]{1,0:T(8,128)S(1)}, u32[]{:S(2)}, u32[]{:S(2)}) collective-permute-start(f32[16,256]{1,0:T(8,128)S(1)} %get-tuple-element.91), channel_id=1, source_target_pairs={{0,1},{1,0},{2,3},{3,2},{4,5},{5,4},{6,7},{7,6},{8,9},{9,8},{10,11... | collective-permute-start | bytes 49160 | tf_op jit(solution)/shard_map/ppermute | solution.py:691
  18.3 6.3 %collective-permute-start.7 = (f32[112,128]{1,0:T(8,128)S(1)}, f32[112,128]{1,0:T(8,128)S(1)}, u32[]{:S(2)}, u32[]{:S(2)}) collective-permute-start(f32[112,128]{1,0:T(8,128)S(1)} %get-tuple-element.104), channel_id=1, source_target_pairs={{0,4},{1,5},{2,6},{3,7},{4,0},{5,1},{6,2},{7,3},{8,12},{9,13},{10,... | collective-permute-start | bytes 172040 | tf_op jit(solution)/shard_map/ppermute | solution.py:692
  21.2 4.0 %collective-permute-start.5 = (f32[112,128]{1,0:T(8,128)S(1)}, f32[112,128]{1,0:T(8,128)S(1)}, u32[]{:S(2)}, u32[]{:S(2)}) collective-permute-start(f32[112,128]{1,0:T(8,128)S(1)} %get-tuple-element.92), channel_id=1, source_target_pairs={{0,1},{1,0},{2,3},{3,2},{4,8},{5,9},{6,10},{7,11},{8,4},{9,5},{10,... | collective-permute-start | bytes 172040 | tf_op jit(solution)/shard_map/ppermute | solution.py:698
  21.4 3.8 %collective-permute-start.6 = (f32[16,256]{1,0:T(8,128)S(1)}, f32[16,256]{1,0:T(8,128)S(1)}, u32[]{:S(2)}, u32[]{:S(2)}) collective-permute-start(f32[16,256]{1,0:T(8,128)S(1)} %pad_maximum_fusion.1), channel_id=1, source_target_pairs={{0,2},{1,3},{2,0},{3,1},{4,6},{5,7},{6,4},{7,5},{8,10},{9,11},{10,... | collective-permute-start | bytes 49160 | tf_op jit(solution)/shard_map/ppermute | solution.py:697

commit v6 on v5

--- a/solution.py
+++ b/solution.py
@@ -305,26 +305,24 @@
         for i in range(GROUP):
             first_ref[g * GROUP + i] = values[i] * HALF
             late_ref[g * GROUP + i] = values[i] * (1.0 - HALF)
-    for copy in copies[4:6]:
-        copy.wait()
     def send_picks():
+        copies[4].wait()
         picks_of_sends(send_ref, pick_ref, pick_sub_ref)
 
     def restrict_left():
+        copies[5].wait()
         rstage_ref[...] = jnp.zeros_like(rstage_ref)
         for f in range(4):
             rstage_ref[f * PAD : f * PAD + restrict_ref.shape[0], :basis] = restrict_ref[:, f, :]
         rleft_ref[...] = stack_left(rstage_ref[:, :basis])
 
-    send_picks()
-    restrict_left()
 
     def finish(p, first):
         first_ref[p] = first
         return first
 
     for g, values in predictor(moved_ref, other_ref, star_ref, left, first_ref, late_ref, sizes, finish,
-                               []):
+                               [send_picks, restrict_left]):
         project(g, values, rleft_ref[...], proj_ref)
     by_face(proj_ref, faces_ref, sizes)
     payloads(faces_ref, pick_ref, pick_sub_ref, slot_ref, (pa_ref, pb_ref, p1_ref, pk_refs), sizes)

time: 26.8 us -> 27 us (level)
  no operation moved by 1% of the time
where the time goes in v6:
time: 27 us; the launch traced here: 26.8 us
  Pallas kernels  17.3 us (64%)
  starting transfers between devices  9.37 us (35%)
    pallas_call x6, Pallas kernels, call(): pl.pallas_call(functools.partial(fn, sizes), out_shape=outs, in_specs=[pl...  17.3 us
    ppermute x2, starting transfers between devices, trade(): ra = lax.ppermute(pa, combined, even_pairs)  5.49 us
    ppermute x2, starting transfers between devices, trade(): lax.ppermute(jnp.concatenate([part, passed], axis=0), combined, sub_pairs...  2.89 us
    ppermute x2, starting transfers between devices, trade(): r1 = lax.ppermute(p1, combined, sub_pairs(1))  0.67 us
  transfers between devices with their start and end apart: 8, of which 0 were waited for; matrix products, arithmetic and copies ran while one was open for 0% of the time, Pallas kernels for 17%

profile of v6, /device:TPU:0, one launch (start us, length us, event | category | flops | bytes accessed | tf_op | source)
XLA Modules:
  0.0 26.8 jit_solution(6034715779283915895)
XLA Ops:
  0.0 6.1 %shard_map.136 = (s32[1,128]{1,0:T(1,128)S(1)}, s32[1,128]{1,0:T(1,128)S(1)}, f32[9,9,4,64]{3,2,1,0:T(4,128)S(1)}, f32[9,9,4,64]{3,2,1,0:T(4,128)S(1)}, s32[4,12...) custom-call(f32[9,56,128]{2,1,0:T(8,128)} %bitcast.10, ...), custom_call_target="tpu_custom_call" | custom-call | flops 60000000 | bytes 2000000 | tf_op jit(solution)/shard_map/pallas_call | solution.py:663
  6.1 0.5 %collective-permute-start.1 = (f32[16,256]{1,0:T(8,128)S(1)}, f32[16,256]{1,0:T(8,128)S(1)}, u32[]{:S(2)}, u32[]{:S(2)}) collective-permute-start(f32[16,256]{1,0:T(8,128)S(1)} %get-tuple-element.58), channel_id=1, source_target_pairs={{0,1},{1,0},{2,3},{3,2},{4,5},{5,4},{6,7},{7,6},{8,9},{9,8},{10,11... | collective-permute-start | bytes 49160 | tf_op jit(solution)/shard_map/ppermute | solution.py:689
  6.6 2.6 %collective-permute-start = (f32[112,128]{1,0:T(8,128)S(1)}, f32[112,128]{1,0:T(8,128)S(1)}, u32[]{:S(2)}, u32[]{:S(2)}) collective-permute-start(f32[112,128]{1,0:T(8,128)S(1)} %get-tuple-element.56), channel_id=1, source_target_pairs={{0,4},{1,5},{2,6},{3,7},{4,0},{5,1},{6,2},{7,3},{8,12},{9,13},{10,... | collective-permute-start | bytes 172040 | tf_op jit(solution)/shard_map/ppermute | solution.py:690
  9.2 0.0 collective-permute-done.1.refs_2_
  9.2 0.2 collective-permute-start.2
  9.4 1.5 %collective-permute-start.3 = (f32[16,256]{1,0:T(8,128)S(1)}, f32[16,256]{1,0:T(8,128)S(1)}, u32[]{:S(2)}, u32[]{:S(2)}) collective-permute-start(f32[16,256]{1,0:T(8,128)S(1)} %pad_maximum_fusion), channel_id=1, source_target_pairs={{0,2},{1,3},{2,0},{3,1},{4,6},{5,7},{6,4},{7,5},{8,10},{9,11},{10,... | collective-permute-start | bytes 49160 | tf_op jit(solution)/shard_map/ppermute | solution.py:695
  10.8 2.3 %shard_map.137 = (f32[9,56,128]{2,1,0:T(8,128)S(1)}, f32[216,512]{1,0:T(8,128)S(1)}, f32[96,1152]{1,0:T(8,128)S(1)}, f32[328,128]{1,0:T(8,128)S(1)}, f32[328,128...) custom-call(s32[1,128]{1,0:T(1,128)S(1)} %get-tuple-element.62.refs_, ...), custom_call_target="tpu_custom_call" | custom-call | flops 30000000 | bytes 2000000 | tf_op jit(solution)/shard_map/pallas_call | solution.py:663
  13.1 0.0 collective-permute-done.3.refs_3_
  13.1 0.0 collective-permute-done.refs_0_
  13.2 0.0 collective-permute-done.2.refs_1_
  13.2 5.2 %shard_map.138 = (f32[9,56,128]{2,1,0:T(8,128)S(1)}, f32[9,56,128]{2,1,0:T(8,128)S(1)}, f32[96,1152]{1,0:T(8,128)S(1)}, bf16[448,512]{1,0:T(8,128)(2,1)S(1)}, f3...) custom-call(f32[112,128]{1,0:T(8,128)S(1)} %collective-permute-done.refs_0_, ...), custom_call_target="tpu_custom_call" | custom-call | flops 70000000 | bytes 2000000 | tf_op jit(solution)/shard_map/pallas_call | solution.py:663
  18.3 0.1 collective-permute-start.4
  18.5 2.9 %collective-permute-start.7 = (f32[112,128]{1,0:T(8,128)S(1)}, f32[112,128]{1,0:T(8,128)S(1)}, u32[]{:S(2)}, u32[]{:S(2)}) collective-permute-start(f32[112,128]{1,0:T(8,128)S(1)} %get-tuple-element.104), channel_id=1, source_target_pairs={{0,4},{1,5},{2,6},{3,7},{4,0},{5,1},{6,2},{7,3},{8,12},{9,13},{10,... | collective-permute-start | bytes 172040 | tf_op jit(solution)/shard_map/ppermute | solution.py:690
  21.4 0.0 collective-permute-done.4.refs_1_
  21.4 0.2 collective-permute-start.5
  21.5 1.4 %collective-permute-start.6 = (f32[16,256]{1,0:T(8,128)S(1)}, f32[16,256]{1,0:T(8,128)S(1)}, u32[]{:S(2)}, u32[]{:S(2)}) collective-permute-start(f32[16,256]{1,0:T(8,128)S(1)} %pad_maximum_fusion.1), channel_id=1, source_target_pairs={{0,2},{1,3},{2,0},{3,1},{4,6},{5,7},{6,4},{7,5},{8,10},{9,11},{10,... | collective-permute-start | bytes 49160 | tf_op jit(solution)/shard_map/ppermute | solution.py:695
  22.9 1.8 %shard_map.139 = (f32[9,56,128]{2,1,0:T(8,128)S(1)}, f32[96,1152]{1,0:T(8,128)S(1)}, f32[96,256]{1,0:T(8,128)S(1)}) custom-call(f32[9,56,128]{2,1,0:T(8,128)S(1)} %get-tuple-element.95.refs_0_, f32[9,56,128]{2,1,0:T(8,128)S(1)} %get-tuple-element.96.refs_1_, f32[328,128]{1,0:T(8,128)S(1)} %get-tuple-element.72.refs_10_.refs_13_.refs_2_, ...), custom_call_target="tpu_custom_call" | custom-call | flops 30000000 | bytes 2000000 | tf_op jit(solution)/shard_map/pallas_call | solution.py:663
  24.8 0.0 collective-permute-done.7.refs_0_
  24.8 0.5 %shard_map.140.refs_7_ = f32[96,1152]{1,0:T(8,128)S(1)} custom-call(f32[112,128]{1,0:T(8,128)S(1)} %collective-permute-done.7.refs_0_, bf16[80,96]{1,0:T(8,128)(2,1)S(1)} %get-tuple-element.75.refs_4_.refs_8_.refs_1_.refs_3_, s32[1,256]{1,0:T(1,128)S(1)} %get-tuple-element.76.refs_5_.refs_2_.refs_4_, ...), custom_call_target="tpu_custom_call" | custom-call | flops 3000000 | bytes 2000000 | tf_op jit(solution)/shard_map/pallas_call | solution.py:663
  25.3 0.0 collective-permute-done.6.refs_2_
  25.3 0.0 collective-permute-done.5.refs_0_
  25.3 1.5 %shard_map.141 = f32[9,56,128]{2,1,0:T(8,128)} custom-call(f32[112,128]{1,0:T(8,128)S(1)} %collective-permute-done.5.refs_0_, f32[16,256]{1,0:T(8,128)S(1)} %collective-permute-done.4.refs_1_, f32[16,256]{1,0:T(8,128)S(1)} %collective-permute-done.6.refs_2_, bf16[80,96]{1,0:T(8,128)(2,1)S(1)} %get-tuple-element.75.refs_4_.refs_8_.refs_1_.refs_3_, ...), custom_call_target="tpu_custom_call" | custom-call | flops 10000000 | bytes 2000000 | tf_op jit(solution)/shard_map/pallas_call | solution.py:663
  (4 shorter events, 0.0 us)
Async XLA Ops:
  6.1 3.1 %collective-permute-start.1 = (f32[16,256]{1,0:T(8,128)S(1)}, f32[16,256]{1,0:T(8,128)S(1)}, u32[]{:S(2)}, u32[]{:S(2)}) collective-permute-start(f32[16,256]{1,0:T(8,128)S(1)} %get-tuple-element.58), channel_id=1, source_target_pairs={{0,1},{1,0},{2,3},{3,2},{4,5},{5,4},{6,7},{7,6},{8,9},{9,8},{10,11... | collective-permute-start | bytes 49160 | tf_op jit(solution)/shard_map/ppermute | solution.py:689
  6.6 6.6 %collective-permute-start = (f32[112,128]{1,0:T(8,128)S(1)}, f32[112,128]{1,0:T(8,128)S(1)}, u32[]{:S(2)}, u32[]{:S(2)}) collective-permute-start(f32[112,128]{1,0:T(8,128)S(1)} %get-tuple-element.56), channel_id=1, source_target_pairs={{0,4},{1,5},{2,6},{3,7},{4,0},{5,1},{6,2},{7,3},{8,12},{9,13},{10,... | collective-permute-start | bytes 172040 | tf_op jit(solution)/shard_map/ppermute | solution.py:690
  9.2 4.0 %collective-permute-start.2 = (f32[112,128]{1,0:T(8,128)S(1)}, f32[112,128]{1,0:T(8,128)S(1)}, u32[]{:S(2)}, u32[]{:S(2)}) collective-permute-start(f32[112,128]{1,0:T(8,128)S(1)} %get-tuple-element.59), channel_id=1, source_target_pairs={{0,1},{1,0},{2,3},{3,2},{4,8},{5,9},{6,10},{7,11},{8,4},{9,5},{10,... | collective-permute-start | bytes 172040 | tf_op jit(solution)/shard_map/ppermute | solution.py:696
  9.4 3.8 %collective-permute-start.3 = (f32[16,256]{1,0:T(8,128)S(1)}, f32[16,256]{1,0:T(8,128)S(1)}, u32[]{:S(2)}, u32[]{:S(2)}) collective-permute-start(f32[16,256]{1,0:T(8,128)S(1)} %pad_maximum_fusion), channel_id=1, source_target_pairs={{0,2},{1,3},{2,0},{3,1},{4,6},{5,7},{6,4},{7,5},{8,10},{9,11},{10,... | collective-permute-start | bytes 49160 | tf_op jit(solution)/shard_map/ppermute | solution.py:695
  18.3 3.0 %collective-permute-start.4 = (f32[16,256]{1,0:T(8,128)S(1)}, f32[16,256]{1,0:T(8,128)S(1)}, u32[]{:S(2)}, u32[]{:S(2)}) collective-permute-start(f32[16,256]{1,0:T(8,128)S(1)} %get-tuple-element.91), channel_id=1, source_target_pairs={{0,1},{1,0},{2,3},{3,2},{4,5},{5,4},{6,7},{7,6},{8,9},{9,8},{10,11... | collective-permute-start | bytes 49160 | tf_op jit(solution)/shard_map/ppermute | solution.py:689
  18.5 6.3 %collective-permute-start.7 = (f32[112,128]{1,0:T(8,128)S(1)}, f32[112,128]{1,0:T(8,128)S(1)}, u32[]{:S(2)}, u32[]{:S(2)}) collective-permute-start(f32[112,128]{1,0:T(8,128)S(1)} %get-tuple-element.104), channel_id=1, source_target_pairs={{0,4},{1,5},{2,6},{3,7},{4,0},{5,1},{6,2},{7,3},{8,12},{9,13},{10,... | collective-permute-start | bytes 172040 | tf_op jit(solution)/shard_map/ppermute | solution.py:690
  21.4 4.0 %collective-permute-start.5 = (f32[112,128]{1,0:T(8,128)S(1)}, f32[112,128]{1,0:T(8,128)S(1)}, u32[]{:S(2)}, u32[]{:S(2)}) collective-permute-start(f32[112,128]{1,0:T(8,128)S(1)} %get-tuple-element.92), channel_id=1, source_target_pairs={{0,1},{1,0},{2,3},{3,2},{4,8},{5,9},{6,10},{7,11},{8,4},{9,5},{10,... | collective-permute-start | bytes 172040 | tf_op jit(solution)/shard_map/ppermute | solution.py:696
  21.5 3.8 %collective-permute-start.6 = (f32[16,256]{1,0:T(8,128)S(1)}, f32[16,256]{1,0:T(8,128)S(1)}, u32[]{:S(2)}, u32[]{:S(2)}) collective-permute-start(f32[16,256]{1,0:T(8,128)S(1)} %pad_maximum_fusion.1), channel_id=1, source_target_pairs={{0,2},{1,3},{2,0},{3,1},{4,6},{5,7},{6,4},{7,5},{8,10},{9,11},{10,... | collective-permute-start | bytes 49160 | tf_op jit(solution)/shard_map/ppermute | solution.py:695
